TPU v7x, 512 devices: a whole 4x8x8 slice. The times are simulated.
512 devices in a mesh: grp: 8 (over z), seg: 64 (over y, x, core).
Axes of the slice: x: 4, y: 8, z: 8, core: 2. Of those that a mesh axis runs over, the one named last changes fastest.
Arguments:
- spectra: bfloat16 [16384, 4096], P(('grp', 'seg')), may hold values from -6 to 6
- gap_counts: int32 [16384], P(('grp', 'seg')), may hold values from 0 to 53999
- band_weight: float32 [2048], replicated, may hold values from 0.1 to 1
- pair_list: int32 [524288, 2], P(('grp', 'seg')), may hold values from 0 to 255, as said below
- stack_owner: int32 [524288, 1], P(('grp', 'seg')), may hold values from 0 to 63; in each aligned block of 1024 rows (0 to 1023, 1024 to 2047, ...) at most 24 rows name the same one
- stack_slot: int32 [524288], P(('grp', 'seg')), may hold values from 0 to 31
Outputs:
- stacked: float32 [16384, 256], P(('grp', 'seg'))
Inputs may be any that keep to these rules, and one draw needn't show every extreme that they name: `stack_owner`: among the rows of one device, at most 24 pairs name the same owner, a bound that some block reaches of them. `pair_list`: the two stations of a pair differ, and no unordered pair of stations appears twice among the rows of one station group.
All inputs are finite; a program needn't handle non-finite values.
Results may differ from a plain program's by a relative error of at most 0.0057.
Values may be sent and summed in bfloat16 or wider, within the bound.
No kernel may reach another device: no remote copies, remote signals or barrier semaphores. Data moves between devices by JAX's collectives and lax.ppermute only.
A program may use at most 64 MiB of HBM per device.

v0:
```python
import math

import jax
import jax.numpy as jnp
from jax import lax
from jax.sharding import PartitionSpec as P

F = 2048
LAGS = 256
SAMPLES = 72000
SLOTS_DEV = 32


def whiten(spectra, gap_counts):
    values = spectra.astype(jnp.float32)
    power = jnp.mean(values * values, axis=1)
    factor = jnp.sqrt(SAMPLES / (SAMPLES - gap_counts.astype(jnp.float32))) / jnp.sqrt(
        power + 1e-06
    )
    return (values * factor[:, None]).astype(jnp.bfloat16)


def make_kernel(band_weight):
    freqs = jnp.arange(F, dtype=jnp.int32)
    shifts = jnp.arange(LAGS, dtype=jnp.int32) - LAGS // 2
    phase_index = freqs[:, None] * shifts[None, :] % (2 * F)
    angles = phase_index.astype(jnp.float32) * (math.pi / F)
    weights = band_weight * (0.25 / math.sqrt(F))
    upper = weights[:, None] * jnp.cos(angles)
    lower = -weights[:, None] * jnp.sin(angles)
    return jnp.concatenate([upper, lower], axis=0).astype(jnp.bfloat16)


def correlate(rows_first, rows_second, kernel):
    half = rows_first.shape[1] // 2
    real_first = rows_first[:, :half]
    imag_first = rows_first[:, half:]
    real_second = rows_second[:, :half]
    imag_second = rows_second[:, half:]
    cross = jnp.concatenate(
        [
            real_first * real_second + imag_first * imag_second,
            imag_first * real_second - real_first * imag_second,
        ],
        axis=1,
    ).astype(jnp.bfloat16)
    return jnp.dot(cross, kernel, preferred_element_type=jnp.float32)


def exact_dot(left, right):
    return jnp.dot(left, right, precision=lax.Precision.HIGHEST, preferred_element_type=jnp.float32)


def on_device(spectra, gap_counts, band_weight, pair_list, stack_owner, stack_slot):
    white = whiten(spectra, gap_counts)
    kernel = make_kernel(band_weight)
    group_rows = lax.all_gather(white, "grp", axis=0, tiled=True)
    group_size = group_rows.shape[0]
    pairs_here = pair_list.shape[0]
    block = min(512, pairs_here)
    blocks = pair_list.reshape(pairs_here // block, block, 2)
    station_ids = jnp.arange(group_size, dtype=jnp.int32)

    def one_block(indices):
        pick_first = (indices[:, 0:1] == station_ids[None, :]).astype(jnp.bfloat16)
        pick_second = (indices[:, 1:2] == station_ids[None, :]).astype(jnp.bfloat16)
        rows_first = jnp.dot(pick_first, group_rows, preferred_element_type=jnp.float32)
        rows_second = jnp.dot(pick_second, group_rows, preferred_element_type=jnp.float32)
        return correlate(rows_first, rows_second, kernel)

    correlation = lax.map(one_block, blocks).reshape(pairs_here, LAGS)
    owners = stack_owner[:, 0]
    seg_count = lax.axis_size("seg")
    capacity = 3 * pairs_here // (2 * seg_count)
    hits = (owners[:, None] == jnp.arange(seg_count, dtype=jnp.int32)[None, :]).astype(jnp.float32)
    row_ids = jnp.arange(pairs_here, dtype=jnp.int32)
    lower_tri = (row_ids[:, None] > row_ids[None, :]).astype(jnp.float32)
    earlier = exact_dot(lower_tri, hits)
    position = jnp.sum(earlier * hits, axis=1).astype(jnp.int32)
    dest = owners * capacity + position
    place = (jnp.arange(seg_count * capacity, dtype=jnp.int32)[:, None] == dest[None, :]).astype(
        jnp.float32
    )
    tile_buffer = exact_dot(place, correlation).reshape(seg_count, capacity, LAGS)
    filled = jnp.sum(place, axis=1)
    slot_values = exact_dot(place, stack_slot.astype(jnp.float32)[:, None])[:, 0]
    slot_buffer = (slot_values + (1.0 - filled) * float(SLOTS_DEV)).reshape(seg_count, capacity)
    got_tiles, got_slots = (
        lax.all_to_all(tile_buffer, "seg", split_axis=0, concat_axis=0, tiled=True),
        lax.all_to_all(slot_buffer, "seg", split_axis=0, concat_axis=0, tiled=True),
    )
    slot_ids = got_slots.reshape(-1).astype(jnp.int32)
    bin_match = (jnp.arange(SLOTS_DEV, dtype=jnp.int32)[:, None] == slot_ids[None, :]).astype(
        jnp.float32
    )
    stacked = exact_dot(bin_match, got_tiles.reshape(-1, LAGS))
    return stacked


def solution(mesh):
    placed = (
        P(("grp", "seg"), None),
        P(("grp", "seg")),
        P(),
        P(("grp", "seg"), None),
        P(("grp", "seg"), None),
        P(("grp", "seg")),
    )
    return jax.shard_map(
        on_device, mesh=mesh, in_specs=placed, out_specs=P(("grp", "seg"), None), check_vma=False
    )
```

profile of v0, /device:TPU:6, one launch (start us, length us, event | category | flops | bytes accessed | tf_op | source)
XLA Modules:
  0.0 137.9 jit_solution(5361801117118613419)
XLA Ops:
  6.5 0.0 copy-start.3
  6.5 0.0 all-gather.2.cloned.1.call-start
  6.5 1.1 fusion.33
  7.7 0.7 rsqrt_multiply_fusion
  8.3 0.0 copy-start.2
  8.3 1.8 %fusion.34 = bf16[32,4096]{1,0:T(8,128)(2,1)} fusion(bf16[32,4096]{1,0:T(8,128)(2,1)} %param.8, f32[32]{0:T(128)S(1)} %rsqrt_multiply_fusion), kind=kLoop, calls=%fused_computation.45 | loop fusion | flops 393216 | bytes 524416 | tf_op jit(solution)/shard_map/convert_element_type | solution.py:20
  10.1 0.0 all-gather.2.cloned.1.call-update
  10.2 0.7 convert_element_type.45
  10.9 1.4 fusion.31
  12.2 0.0 copy-done.3
  12.2 2.9 %fusion.32 = f32[1536]{0:T(1024)S(1)} fusion(f32[1024,1]{0,1:T(1,128)S(1)} %bitcast.42, s32[1024]{0:T(1024)S(1)} %convert_add_fusion), kind=kOutput, calls=%fused_computation.41 | convolution fusion | flops 20447232 | bytes 14336 | tf_op jit(solution)/shard_map/dot_general | solution.py:51
  15.1 0.7 convert_reduce_fusion
  15.8 0.7 add.52
  16.5 10.6 %all-to-all-start = ((f32[64,1,24]{2,1,0:T(1,128)}), f32[64,1,24]{2,1,0:T(1,128)S(1)}, u32[]{:S(2)}, u32[]{:S(2)}) async-start(f32[64,1,24]{2,1,0:T(1,128)} %bitcast.2), calls=%async_computation | async-start | bytes 65536 | tf_op jit(solution)/shard_map/all_to_all | solution.py:90
  27.2 0.0 copy-done.2
  27.2 9.2 %multiply_convert_fusion.1 = (bf16[2048,256]{1,0:T(8,128)(2,1)S(1)}, bf16[2048,256]{1,0:T(8,128)(2,1)S(1)}) fusion(s32[256]{0:T(256)S(1)} %iota_add_fusion, f32[2048]{0:T(1024)S(1)} %get-tuple-element.83, f32[2048]{0:T(1024)S(1)} %get-tuple-element.84), kind=kLoop, calls=%fused_computation.35 | loop fusion | flops 9437184 | bytes 2114560 | tf_op jit(solution)/shard_map/convert.2
  36.4 0.0 copy-start.1
  36.4 0.1 pad_maximum_fusion
  36.5 23.0 %all-gather.2.cloned.1.call-done = bf16[256,4096]{1,0:T(8,128)(2,1)} async-done(((bf16[32,4096]{1,0:T(8,128)(2,1)}), bf16[256,4096]{1,0:T(8,128)(2,1)}) %all-gather.2.cloned.1.call-update) | async-done | bytes 2097168 | tf_op jit(solution)/shard_map/all_gather | solution.py:57
  59.6 0.0 copy-done.1
  59.6 15.9 %while.12 = (s32[]{:T(128)}, f32[2,512,256]{2,1,0:T(8,128)S(1)}, s32[2,512,2]{1,2,0:T(2,128)S(1)}, bf16[256,4096]{1,0:T(8,128)(2,1)}, bf16[4096,256]{1,0:T(8,128)(2,1)S(1)}, /*index=5*/s32[]{:T(128)}) while((s32[]{:T(128)}, f32[2,512,256]{2,1,0:T(8,128)S(1)}, s32[2,512,2]{1,2,0:T(2,128)S(1)}, ...), condition=%wide.region_4.5_spmd.clone.clone, body=%wide.region_3.4_spmd.clone.clone.sunk | while | flops 3238264832 | bytes 57167976 | solution.py:71
  59.6 0.0 copy-start
  59.6 3.0 %fusion.59 = f32[512,4096]{1,0:T(8,128)S(1)} fusion(bf16[256,4096]{1,0:T(8,128)(2,1)} %get-tuple-element.141, s32[512]{0:T(512)S(1)} %bitcast.38), kind=kOutput, calls=%fused_computation.12.clone.1 | convolution fusion | flops 1073872896 | bytes 10487808 | tf_op jit(solution)/shard_map/while/body/eval_jaxpr/dot_general | solution.py:68
  62.6 0.0 copy-done
  62.6 1.3 fusion.60
  63.9 2.2 %add_convert_fusion.2 = (bf16[512,2048]{1,0:T(8,128)(2,1)S(1)}, bf16[512,2048]{1,0:T(8,128)(2,1)S(1)}) fusion(f32[512,4096]{1,0:T(8,128)S(1)} %fusion.59, f32[512,4096]{1,0:T(8,128)S(1)} %fusion.60), kind=kLoop, calls=%fused_computation.6.clone.1 | loop fusion | flops 8388608 | bytes 20971520 | tf_op jit(solution)/shard_map/convert
  66.2 1.3 fusion.61
  67.5 0.0 copy-start
  67.5 3.0 %fusion.59 = f32[512,4096]{1,0:T(8,128)S(1)} fusion(bf16[256,4096]{1,0:T(8,128)(2,1)} %get-tuple-element.141, s32[512]{0:T(512)S(1)} %bitcast.38), kind=kOutput, calls=%fused_computation.12.clone.1 | convolution fusion | flops 1073872896 | bytes 10487808 | tf_op jit(solution)/shard_map/while/body/eval_jaxpr/dot_general | solution.py:68
  70.6 0.0 copy-done
  70.6 1.3 fusion.60
  71.9 2.2 %add_convert_fusion.2 = (bf16[512,2048]{1,0:T(8,128)(2,1)S(1)}, bf16[512,2048]{1,0:T(8,128)(2,1)S(1)}) fusion(f32[512,4096]{1,0:T(8,128)S(1)} %fusion.59, f32[512,4096]{1,0:T(8,128)S(1)} %fusion.60), kind=kLoop, calls=%fused_computation.6.clone.1 | loop fusion | flops 8388608 | bytes 20971520 | tf_op jit(solution)/shard_map/convert
  74.1 1.3 fusion.61
  75.4 4.0 %fusion.18 = f32[64,24,256]{2,1,0:T(8,128)} fusion(f32[1024,256,1]{1,0,2:T(8,128)S(1)} %bitcast.43, s32[1024]{0:T(1024)S(1)} %convert_add_fusion, s32[64,24]{1,0:T(8,128)S(1)} %multiply_add_fusion), kind=kOutput, calls=%fused_computation.20 | convolution fusion | flops 4833411072 | bytes 2631680 | tf_op jit(solution)/shard_map/dot_general | solution.py:51
  79.5 0.0 all-to-all-done
  79.5 10.3 %all-to-all-start.1 = ((f32[64,24,256]{2,1,0:T(8,128)}), f32[64,24,256]{2,1,0:T(8,128)S(1)}, u32[]{:S(2)}, u32[]{:S(2)}) async-start(f32[64,24,256]{2,1,0:T(8,128)} %fusion.18), calls=%async_computation.1 | async-start | bytes 3145728 | tf_op jit(solution)/shard_map/all_to_all | solution.py:89
  89.7 0.1 convert_reduce_fusion.1
  89.8 0.1 convert_element_type.48
  89.9 39.9 %all-to-all-done.1 = f32[64,24,256]{2,1,0:T(8,128)S(1)} async-done(((f32[64,24,256]{2,1,0:T(8,128)}), f32[64,24,256]{2,1,0:T(8,128)S(1)}, u32[]{:S(2)}, u32[]{:S(2)}) %all-to-all-start.1) | async-done | bytes 1572896 | tf_op jit(solution)/shard_map/all_to_all | solution.py:89
  129.8 1.3 fusion.35
  (10 shorter events, 0.1 us)
Async XLA Ops:
  6.5 5.7 %copy-start.3 = (s32[1024,1]{0,1:T(1,128)S(1)}, s32[1024,1]{0,1:T(1,128)}, u32[]{:S(2)}) copy-start(s32[1024,1]{0,1:T(1,128)} %param.12) | copy-start | bytes 12292
  6.5 53.0 %all-gather.2.cloned.1.call-start = ((), (), s32[]{:S(2)}) async-start(), calls=%async_computation.2 | async-start | bytes 2359296 | tf_op jit(solution)/shard_map/all_gather | solution.py:57
  8.3 18.9 %copy-start.2 = (f32[2048]{0:T(1024)S(1)}, f32[2048]{0:T(1024)}, u32[]{:S(2)}) copy-start(f32[2048]{0:T(1024)} %param.10) | copy-start | bytes 24580
  16.5 62.9 %all-to-all-start = ((f32[64,1,24]{2,1,0:T(1,128)}), f32[64,1,24]{2,1,0:T(1,128)S(1)}, u32[]{:S(2)}, u32[]{:S(2)}) async-start(f32[64,1,24]{2,1,0:T(1,128)} %bitcast.2), calls=%async_computation | async-start | bytes 65536 | tf_op jit(solution)/shard_map/all_to_all | solution.py:90
  36.4 23.2 %copy-start.1 = (s32[1024,2]{0,1:T(2,128)S(1)}, s32[1024,2]{0,1:T(2,128)}, u32[]{:S(2)}) copy-start(s32[1024,2]{0,1:T(2,128)} %param.11) | copy-start | bytes 24580
  59.6 3.1 %copy-start = (bf16[256,4096]{1,0:T(8,128)(2,1)S(1)}, bf16[256,4096]{1,0:T(8,128)(2,1)}, u32[]{:S(2)}) copy-start(bf16[256,4096]{1,0:T(8,128)(2,1)} %get-tuple-element.141) | copy-start | bytes 6291460 | tf_op jit(solution)/shard_map/while
  67.5 3.1 %copy-start = (bf16[256,4096]{1,0:T(8,128)(2,1)S(1)}, bf16[256,4096]{1,0:T(8,128)(2,1)}, u32[]{:S(2)}) copy-start(bf16[256,4096]{1,0:T(8,128)(2,1)} %get-tuple-element.141) | copy-start | bytes 6291460 | tf_op jit(solution)/shard_map/while
  79.5 50.3 %all-to-all-start.1 = ((f32[64,24,256]{2,1,0:T(8,128)}), f32[64,24,256]{2,1,0:T(8,128)S(1)}, u32[]{:S(2)}, u32[]{:S(2)}) async-start(f32[64,24,256]{2,1,0:T(8,128)} %fusion.18), calls=%async_computation.1 | async-start | bytes 3145728 | tf_op jit(solution)/shard_map/all_to_all | solution.py:89
Sparse Core Ops, SparseCore 0:
  10.3 49.2 all-gather.1
where the time goes:
time: 138 us
  waiting for transfers between devices  62.9 us (46%)
  starting transfers between devices  20.9 us (15%)
  matrix products  20.8 us (15%)
  other arithmetic  18.9 us (14%)
  between operations  13.5 us (10%)
    all_to_all x1, waiting for transfers between devices, on_device(): lax.all_to_all(tile_buffer, 'seg', split_axis=0, concat_axis=0, tiled=True)  39.9 us
    all_gather x1, waiting for transfers between devices, on_device(): group_rows = lax.all_gather(white, 'grp', axis=0, tiled=True)  23 us
    another operation x3, other arithmetic  13.7 us
    all_to_all x1, starting transfers between devices, on_device(): lax.all_to_all(slot_buffer, 'seg', split_axis=0, concat_axis=0, tiled=True)  10.6 us
    all_to_all x1, starting transfers between devices, on_device(): lax.all_to_all(tile_buffer, 'seg', split_axis=0, concat_axis=0, tiled=True)  10.3 us
    dot_general x4, matrix products, exact_dot(): jnp.dot(left, right, precision=lax.Precision.HIGHEST, preferred_element_t...  9.53 us
    dot_general x2, matrix products, one_block(): jnp.dot(pick_second, group_rows, preferred_element_type=jnp.float32)  6.07 us
  transfers between devices with their start and end apart: 3, of which 2 were waited for; matrix products, arithmetic and copies ran while one was open for 26% of the time, Pallas kernels for 0%

commit v1 on v0

v1 whole, which is shorter than its diff:
```python
import math

import jax
import jax.numpy as jnp
import numpy as np
from jax import lax
from jax.experimental import pallas as pl
from jax.experimental.pallas import tpu as pltpu
from jax.sharding import PartitionSpec as P

F = 2048
LAGS = 256
SAMPLES = 72000
SLOTS_DEV = 32
LIFT = 256.0
CHUNK = 512
ROWS = 256
VMEM = 56 * 1024 * 1024


def tables():
    freqs = np.arange(F, dtype=np.int64)
    shifts = np.arange(LAGS, dtype=np.int64) - LAGS // 2
    angles = ((shifts[:, None] * freqs[None, :]) % (2 * F)).astype(np.float64) * (math.pi / F)
    return np.cos(angles).astype(np.float32), (-np.sin(angles)).astype(np.float32)


def whiten_kernel(spectra_ref, gap_ref, out_ref):
    values = spectra_ref[...].astype(jnp.float32)
    power = jnp.mean(values * values, axis=1, keepdims=True)
    kept = SAMPLES - gap_ref[...].astype(jnp.float32)
    factor = jnp.sqrt(SAMPLES / kept) / jnp.sqrt(power + 1e-06)
    out_ref[...] = (values * factor).astype(jnp.bfloat16) * LIFT


def pick_bins(owner_ref, slot_ref, parity):
    owner = owner_ref[...]
    local = (owner >> 1) * SLOTS_DEV + slot_ref[...]
    return jnp.where((owner & 1) == parity, local, -1)


def into_bins(bins, corr_ref, out_ref):
    pairs = corr_ref.shape[0]
    count = out_ref.shape[0]
    for start in range(0, count, ROWS):
        ids = lax.broadcasted_iota(jnp.int32, (ROWS, pairs), 0) + start
        place = (ids == bins).astype(jnp.bfloat16)
        out_ref[start : start + ROWS, :] = jnp.dot(
            place, corr_ref[...], preferred_element_type=jnp.float32
        ).astype(out_ref.dtype)


def correlate_kernel(
    pairs_ref, owner_ref, slot_ref, real_ref, imag_ref, weight_ref, cos_ref, sin_ref,
    corr_ref, away_ref, first_ref, second_ref, total_ref,
):
    step = pl.program_id(0)
    group = real_ref.shape[0]
    pairs = total_ref.shape[0]

    @pl.when(step == 0)
    def _():
        ids = lax.broadcasted_iota(jnp.int32, (group, pairs), 0)
        first_ref[...] = (ids == pairs_ref[0:1, :]).astype(jnp.float32).T.astype(jnp.bfloat16)
        second_ref[...] = (ids == pairs_ref[1:2, :]).astype(jnp.float32).T.astype(jnp.bfloat16)
        total_ref[...] = jnp.zeros_like(total_ref)

    weight = weight_ref[...] * (0.25 / math.sqrt(F) / (LIFT * LIFT))
    upper = (weight * cos_ref[...]).astype(jnp.bfloat16)
    lower = (weight * sin_ref[...]).astype(jnp.bfloat16)
    real = real_ref[...]
    imag = imag_ref[...]

    def pick(one_hot, rows):
        return jnp.dot(one_hot, rows, preferred_element_type=jnp.float32)

    def lags(cross, table):
        return lax.dot_general(
            cross.astype(jnp.bfloat16), table, (((1,), (1,)), ((), ())),
            preferred_element_type=jnp.float32,
        )

    for start in range(0, pairs, ROWS):
        rows = slice(start, start + ROWS)
        one, two = first_ref[rows, :], second_ref[rows, :]
        real_one, imag_one = pick(one, real), pick(one, imag)
        real_two, imag_two = pick(two, real), pick(two, imag)
        total_ref[rows, :] += lags(real_one * real_two + imag_one * imag_two, upper) + lags(
            imag_one * real_two - real_one * imag_two, lower
        )

    @pl.when(step == pl.num_programs(0) - 1)
    def _():
        corr_ref[...] = total_ref[...].astype(jnp.bfloat16)
        core = lax.axis_index("seg") & 1
        into_bins(pick_bins(owner_ref, slot_ref, 1 - core), corr_ref, away_ref)


def own_kernel(owner_ref, slot_ref, corr_ref, out_ref):
    core = lax.axis_index("seg") & 1
    into_bins(pick_bins(owner_ref, slot_ref, core), corr_ref, out_ref)


def on_device(spectra, gap_counts, band_weight, pair_list, stack_owner, stack_slot):
    stations = spectra.shape[0]
    pairs = pair_list.shape[0]
    seg = lax.axis_size("seg")
    group = stations * lax.axis_size("grp")
    bins = seg // 2 * SLOTS_DEV
    steps = F // CHUNK
    params = pltpu.CompilerParams(vmem_limit_bytes=VMEM)
    white = pl.pallas_call(
        whiten_kernel, out_shape=jax.ShapeDtypeStruct(spectra.shape, jnp.bfloat16), compiler_params=params
    )(spectra, gap_counts.reshape(stations, 1))
    group_rows = lax.all_gather(white.astype(jnp.float16), "grp", axis=0, tiled=True).astype(jnp.bfloat16)

    owner = stack_owner.reshape(1, pairs)
    slot = stack_slot.reshape(1, pairs)
    cos_table, sin_table = tables()
    whole = lambda rows, columns: pl.BlockSpec((rows, columns), lambda i: (0, 0))
    corr, away = pl.pallas_call(
        correlate_kernel,
        grid=(steps,),
        in_specs=[
            whole(2, pairs),
            whole(1, pairs),
            whole(1, pairs),
            pl.BlockSpec((group, CHUNK), lambda i: (0, i)),
            pl.BlockSpec((group, CHUNK), lambda i: (0, i + steps)),
            pl.BlockSpec((1, CHUNK), lambda i: (0, i)),
            pl.BlockSpec((LAGS, CHUNK), lambda i: (0, i)),
            pl.BlockSpec((LAGS, CHUNK), lambda i: (0, i)),
        ],
        out_specs=[whole(pairs, LAGS), whole(bins, LAGS)],
        out_shape=[
            jax.ShapeDtypeStruct((pairs, LAGS), jnp.bfloat16),
            jax.ShapeDtypeStruct((bins, LAGS), jnp.bfloat16),
        ],
        scratch_shapes=[
            pltpu.VMEM((pairs, group), jnp.bfloat16),
            pltpu.VMEM((pairs, group), jnp.bfloat16),
            pltpu.VMEM((pairs, LAGS), jnp.float32),
        ],
        compiler_params=params,
    )(
        pair_list.T, owner, slot, group_rows, group_rows, band_weight.reshape(1, F), cos_table, sin_table
    )
    arrived = lax.ppermute(away, "seg", [(i, i ^ 1) for i in range(seg)])
    kept = pl.pallas_call(
        own_kernel,
        out_shape=jax.ShapeDtypeStruct((bins, LAGS), jnp.float32),
        compiler_params=params,
        cost_estimate=pl.CostEstimate(flops=2 * bins * pairs * LAGS, bytes_accessed=2 << 20, transcendentals=0),
    )(owner, slot, corr)
    chip = (kept + arrived.astype(jnp.float32)).astype(jnp.bfloat16).reshape(seg // 2, SLOTS_DEV, LAGS)
    got = lax.all_to_all(
        chip, "seg", split_axis=0, concat_axis=0, tiled=True,
        axis_index_groups=[list(range(core, seg, 2)) for core in range(2)],
    )
    return jnp.sum(got.astype(jnp.float32), axis=0)


def solution(mesh):
    placed = (
        P(("grp", "seg"), None),
        P(("grp", "seg")),
        P(),
        P(("grp", "seg"), None),
        P(("grp", "seg"), None),
        P(("grp", "seg")),
    )
    return jax.shard_map(
        on_device, mesh=mesh, in_specs=placed, out_specs=P(("grp", "seg"), None), check_vma=False
    )
```

time: 138 us -> 90 us (0.65)
  blocking collectives: 0 us -> 63.8 us
  waiting for transfers between devices: 62.9 us -> 0.01 us
  matrix products: 20.8 us -> 0 us
  starting transfers between devices: 20.9 us -> 1.91 us
  Pallas kernels: 0 us -> 17.8 us
  other arithmetic: 18.9 us -> 4.65 us
  between operations: 13.5 us -> 0.02 us
    all_to_all x2 -> x0, waiting for transfers between devices: 39.9 us -> none  [the longest x1 39.9 us: on_device(): lax.all_to_all(tile_buffer, 'seg', split_axis=0, concat_axis=0, tiled=True)]
    all_gather x0 -> x1, blocking collectives: none -> 36.3 us  [on_device(): lax.all_gather(white.astype(jnp.float16), 'grp', axis=0, tiled=True)]
    all_to_all x0 -> x1, blocking collectives: none -> 27.5 us  [on_device(): lax.all_to_all(chip, 'seg', split_axis=0, concat_axis=0, tiled=True, axis...]
    all_gather x1 -> x0, waiting for transfers between devices: 23 us -> none  [on_device(): group_rows = lax.all_gather(white, 'grp', axis=0, tiled=True)]
    all_to_all x2 -> x0, starting transfers between devices: 20.9 us -> none  [the longest x1 10.6 us: on_device(): lax.all_to_all(slot_buffer, 'seg', split_axis=0, concat_axis=0, tiled=True)]
    dot_general x10 -> x0, matrix products: 20.8 us -> none  [the longest x4 9.53 us: exact_dot(): jnp.dot(left, right, precision=lax.Precision.HIGHEST, preferred_element_t...]
    pallas_call x0 -> x3, Pallas kernels: none -> 17.8 us  [the longest x1 13.1 us: on_device(): pl.pallas_call(correlate_kernel, grid=(steps,), in_specs=[whole(2, pairs)...]
    another operation x3 -> x0, other arithmetic: 13.7 us -> none
  transfers between devices with their start and end apart: 3 -> 1, of which waited for: 2 -> 0; matrix products, arithmetic and copies ran while one was open for 26% -> 0% of each run, Pallas kernels for 0% -> 3%
where the time goes in v1:
time: 90 us; the launch traced here: 89.5 us
  blocking collectives  63.8 us (71%)
  Pallas kernels  17.8 us (20%)
  other arithmetic  4.65 us (5%)
  starting transfers between devices  1.91 us (2%)
  local copies, waits for them, and re-layouts  1.34 us (1%)
    all_gather x1, blocking collectives, on_device(): lax.all_gather(white.astype(jnp.float16), 'grp', axis=0, tiled=True)  36.3 us
    all_to_all x1, blocking collectives, on_device(): lax.all_to_all(chip, 'seg', split_axis=0, concat_axis=0, tiled=True, axis...  27.5 us
    pallas_call x1, Pallas kernels, on_device(): pl.pallas_call(correlate_kernel, grid=(steps,), in_specs=[whole(2, pairs)...  13.1 us
    pallas_call x1, Pallas kernels, on_device(): pl.pallas_call(own_kernel, out_shape=jax.ShapeDtypeStruct((bins, LAGS), j...  2.77 us
    pallas_call x1, Pallas kernels, on_device(): pl.pallas_call(whiten_kernel, out_shape=jax.ShapeDtypeStruct(spectra.shap...  1.94 us
    ppermute x1, starting transfers between devices, on_device(): arrived = lax.ppermute(away, 'seg', [(i, i ^ 1) for i in range(seg)])  1.91 us
  transfers between devices with their start and end apart: 1, of which 0 were waited for; matrix products, arithmetic and copies ran while one was open for 0% of the time, Pallas kernels for 3%

profile of v1, /device:TPU:6, one launch (start us, length us, event | category | flops | bytes accessed | tf_op | source)
XLA Modules:
  0.0 89.5 jit_solution(9194613786323003264)
XLA Ops:
  0.0 1.3 %copy.9.gap_ref = s32[32,1]{1,0:T(8,128)} copy(s32[32,1]{0,1:T(1,128)} %bitcast.13) | data formatting | bytes 256 | tf_op jit(solution)/shard_map/reshape | solution.py:114
  1.3 1.9 %shard_map.82 = bf16[32,4096]{1,0:T(8,128)(2,1)} custom-call(bf16[32,4096]{1,0:T(8,128)(2,1)} %spectra_ref.1, s32[32,1]{1,0:T(8,128)} %copy.9.gap_ref), custom_call_target="tpu_custom_call" | custom-call | tf_op jit(solution)/shard_map/pallas_call | solution.py:112
  3.3 1.0 %convert_element_type.15 = f16[32,4096]{1,0:T(8,128)(2,1)S(1)} convert(bf16[32,4096]{1,0:T(8,128)(2,1)} %shard_map.82) | non-fusion elementwise | flops 131072 | bytes 524288 | tf_op jit(solution)/shard_map/convert_element_type | solution.py:115
  4.3 36.3 %all-gather.1 = f16[256,4096]{1,0:T(8,128)(2,1)S(1)} all-gather(f16[32,4096]{1,0:T(8,128)(2,1)S(1)} %convert_element_type.15), channel_id=1, replica_groups=mesh['grp'=8,'seg'=64] {'grp'}, dimensions={0}, use_global_device_ids=true | all-gather | bytes 2359296 | tf_op jit(solution)/shard_map/all_gather | solution.py:115
  40.6 1.6 %convert_element_type.16.real_ref.imag_ref = bf16[256,4096]{1,0:T(8,128)(2,1)} convert(f16[256,4096]{1,0:T(8,128)(2,1)S(1)} %all-gather.1) | non-fusion elementwise | flops 1048576 | bytes 4194304 | tf_op jit(solution)/shard_map/convert_element_type | solution.py:115
  42.2 13.1 %shard_map.83 = (bf16[1024,256]{1,0:T(8,128)(2,1)}, bf16[1024,256]{1,0:T(8,128)(2,1)}) custom-call(s32[2,1024]{1,0:T(2,128)} %bitcast.7, s32[1,1024]{1,0:T(1,128)} %bitcast.9, s32[1,1024]{1,0:T(1,128)} %bitcast.11, bf16[256,4096]{1,0:T(8,128)(2,1)} %convert_element_type.16.real_ref.imag_ref, bf16[256,4096]{1,0:T(8,128)(2,1)} %convert_element_type.16.real_ref.imag_ref, ...), custom_call_target="tpu_custom_call" | custom-call | tf_op jit(solution)/shard_map/pallas_call | solution.py:121
  55.3 1.9 %collective-permute-start = (bf16[1024,256]{1,0:T(8,128)(2,1)}, bf16[1024,256]{1,0:T(8,128)(2,1)S(1)}, u32[]{:S(2)}, u32[]{:S(2)}) collective-permute-start(bf16[1024,256]{1,0:T(8,128)(2,1)} %get-tuple-element.8), channel_id=1, source_target_pairs={{0,1},{1,0},{2,3},{3,2},{4,5},{5,4},{6,7},{7,6},{8,9},{9,8},{10,11... | collective-permute-start | bytes 1572872 | tf_op jit(solution)/shard_map/ppermute | solution.py:148
  57.2 2.8 %shard_map.84 = f32[1024,256]{1,0:T(8,128)} custom-call(s32[1,1024]{1,0:T(1,128)} %bitcast.10, s32[1,1024]{1,0:T(1,128)} %bitcast.12, bf16[1024,256]{1,0:T(8,128)(2,1)} %get-tuple-element.7.corr_ref), custom_call_target="tpu_custom_call" | custom-call | flops 536870912 | bytes 2097152 | tf_op jit(solution)/shard_map/pallas_call | solution.py:149
  59.9 0.0 collective-permute-done
  59.9 1.3 %add_convert_fusion = bf16[1024,256]{1,0:T(8,128)(2,1)S(1)} fusion(f32[1024,256]{1,0:T(8,128)} %shard_map.84, bf16[1024,256]{1,0:T(8,128)(2,1)S(1)} %collective-permute-done), kind=kLoop, calls=%fused_computation.1 | loop fusion | flops 786432 | bytes 2097152 | tf_op jit(solution)/shard_map/convert_element_type | solution.py:155
  61.3 27.5 %all_to_all.5 = bf16[32,32,256]{2,1,0:T(8,128)(2,1)S(1)} all-to-all(bf16[32,32,256]{2,1,0:T(8,128)(2,1)S(1)} %bitcast.6), channel_id=1, replica_groups={{0,2,4,6,8,10,12,14,16,18,20,22,24,26,28,30,32,34,36,38,40,42,44,46,48,..., dimensions={0} | all-to-all | bytes 1048576 | tf_op jit(solution)/shard_map/all_to_all | solution.py:156
  88.8 0.7 convert_reduce_fusion
Async XLA Ops:
  55.3 4.7 %collective-permute-start = (bf16[1024,256]{1,0:T(8,128)(2,1)}, bf16[1024,256]{1,0:T(8,128)(2,1)S(1)}, u32[]{:S(2)}, u32[]{:S(2)}) collective-permute-start(bf16[1024,256]{1,0:T(8,128)(2,1)} %get-tuple-element.8), channel_id=1, source_target_pairs={{0,1},{1,0},{2,3},{3,2},{4,5},{5,4},{6,7},{7,6},{8,9},{9,8},{10,11... | collective-permute-start | bytes 1572872 | tf_op jit(solution)/shard_map/ppermute | solution.py:148

commit v2 on v1

v2 whole, which is shorter than its diff:
```python
import math

import jax
import jax.numpy as jnp
import numpy as np
from jax import lax
from jax.experimental import pallas as pl
from jax.experimental.pallas import tpu as pltpu
from jax.sharding import PartitionSpec as P

F = 2048
LAGS = 256
SAMPLES = 72000
SLOTS_DEV = 32
LIFT = 256.0
COLUMNS = 256
ROWS = 512
BIN_ROWS = 256
MIB = 1024 * 1024


def tables():
    freqs = np.arange(F, dtype=np.int64)
    shifts = np.arange(LAGS, dtype=np.int64) - LAGS // 2
    angles = ((shifts[:, None] * freqs[None, :]) % (2 * F)).astype(np.float64) * (math.pi / F)
    return np.cos(angles).astype(np.float32), (-np.sin(angles)).astype(np.float32)


def whiten_kernel(spectra_ref, gap_ref, out_ref):
    stations = spectra_ref.shape[0]
    values = spectra_ref[...].astype(jnp.float32)
    power = jnp.mean(values * values, axis=1, keepdims=True)
    kept = jnp.broadcast_to(SAMPLES - gap_ref[...].astype(jnp.float32), (stations, stations))
    here = lax.broadcasted_iota(jnp.int32, (stations, stations), 0)
    along = lax.broadcasted_iota(jnp.int32, (stations, stations), 1)
    kept = jnp.sum(jnp.where(here == along, kept, 0.0), axis=1, keepdims=True)
    factor = jnp.sqrt(SAMPLES / kept) / jnp.sqrt(power + 1e-06)
    out_ref[...] = (values * factor).astype(jnp.bfloat16) * LIFT


def pick_bins(owner_ref, slot_ref, parity):
    owner = owner_ref[...]
    local = (owner >> 1) * SLOTS_DEV + slot_ref[...]
    return jnp.where((owner & 1) == parity, local, -1)


def into_bins(bins, corr_ref, out_ref):
    pairs = corr_ref.shape[0]
    count = out_ref.shape[0]
    for start in range(0, count, BIN_ROWS):
        ids = lax.broadcasted_iota(jnp.int32, (BIN_ROWS, pairs), 0) + start
        place = (ids == bins).astype(jnp.bfloat16)
        out_ref[start : start + BIN_ROWS, :] = jnp.dot(
            place, corr_ref[...], preferred_element_type=jnp.float32
        ).astype(out_ref.dtype)


def correlate_kernel(
    pairs_ref, owner_ref, slot_ref, white_ref, weight_ref, cos_ref, sin_ref,
    corr_ref, away_ref, first_ref, second_ref, upper_ref, lower_ref,
):
    group = white_ref.shape[0]
    pairs = corr_ref.shape[0]
    ids = lax.broadcasted_iota(jnp.int32, (group, pairs), 0)
    first_ref[...] = (ids == pairs_ref[0:1, :]).astype(jnp.float32).T.astype(jnp.bfloat16)
    second_ref[...] = (ids == pairs_ref[1:2, :]).astype(jnp.float32).T.astype(jnp.bfloat16)
    weight = weight_ref[...] * (0.25 / math.sqrt(F) / (LIFT * LIFT))
    upper_ref[...] = (weight * cos_ref[...]).astype(jnp.bfloat16)
    lower_ref[...] = (weight * sin_ref[...]).astype(jnp.bfloat16)

    def pick(one_hot, rows):
        return jnp.dot(one_hot, rows, preferred_element_type=jnp.float32)

    def lags(cross, table):
        return lax.dot_general(
            cross.astype(jnp.bfloat16), table, (((1,), (1,)), ((), ())),
            preferred_element_type=jnp.float32,
        )

    for start in range(0, pairs, ROWS):
        rows = slice(start, start + ROWS)
        one, two = first_ref[rows, :], second_ref[rows, :]
        total = jnp.zeros((ROWS, LAGS), jnp.float32)
        for column in range(0, F, COLUMNS):
            here = slice(column, column + COLUMNS)
            real = white_ref[:, here]
            imag = white_ref[:, F + column : F + column + COLUMNS]
            real_one, imag_one = pick(one, real), pick(one, imag)
            real_two, imag_two = pick(two, real), pick(two, imag)
            total += lags(real_one * real_two + imag_one * imag_two, upper_ref[:, here]) + lags(
                imag_one * real_two - real_one * imag_two, lower_ref[:, here]
            )
        corr_ref[rows, :] = total.astype(jnp.bfloat16)
    core = lax.axis_index("seg") & 1
    into_bins(pick_bins(owner_ref, slot_ref, 1 - core), corr_ref, away_ref)


def own_kernel(owner_ref, slot_ref, corr_ref, out_ref):
    core = lax.axis_index("seg") & 1
    into_bins(pick_bins(owner_ref, slot_ref, core), corr_ref, out_ref)


def on_device(spectra, gap_counts, band_weight, pair_list, stack_owner, stack_slot):
    stations = spectra.shape[0]
    pairs = pair_list.shape[0]
    seg = lax.axis_size("seg")
    group = stations * lax.axis_size("grp")
    bins = seg // 2 * SLOTS_DEV
    white = pl.pallas_call(
        whiten_kernel,
        out_shape=jax.ShapeDtypeStruct(spectra.shape, jnp.bfloat16),
        compiler_params=pltpu.CompilerParams(vmem_limit_bytes=8 * MIB),
    )(spectra, gap_counts.reshape(1, stations))
    group_rows = lax.all_gather(white.astype(jnp.float16), "grp", axis=0, tiled=True).astype(jnp.bfloat16)

    owner = stack_owner.reshape(1, pairs)
    slot = stack_slot.reshape(1, pairs)
    cos_table, sin_table = tables()
    corr, away = pl.pallas_call(
        correlate_kernel,
        out_shape=[
            jax.ShapeDtypeStruct((pairs, LAGS), jnp.bfloat16),
            jax.ShapeDtypeStruct((bins, LAGS), jnp.bfloat16),
        ],
        scratch_shapes=[
            pltpu.VMEM((pairs, group), jnp.bfloat16),
            pltpu.VMEM((pairs, group), jnp.bfloat16),
            pltpu.VMEM((LAGS, F), jnp.bfloat16),
            pltpu.VMEM((LAGS, F), jnp.bfloat16),
        ],
        compiler_params=pltpu.CompilerParams(vmem_limit_bytes=24 * MIB),
    )(
        pair_list.T, owner, slot, group_rows, band_weight.reshape(1, F), cos_table, sin_table
    )
    arrived = lax.ppermute(away, "seg", [(i, i ^ 1) for i in range(seg)])
    kept = pl.pallas_call(
        own_kernel,
        out_shape=jax.ShapeDtypeStruct((bins, LAGS), jnp.float32),
        compiler_params=pltpu.CompilerParams(vmem_limit_bytes=8 * MIB),
        cost_estimate=pl.CostEstimate(flops=2 * bins * pairs * LAGS, bytes_accessed=2 << 20, transcendentals=0),
    )(owner, slot, corr)
    chip = (kept + arrived.astype(jnp.float32)).astype(jnp.bfloat16).reshape(seg // 2, SLOTS_DEV, LAGS)
    got = lax.all_to_all(
        chip, "seg", split_axis=0, concat_axis=0, tiled=True,
        axis_index_groups=[list(range(core, seg, 2)) for core in range(2)],
    )
    return jnp.sum(got.astype(jnp.float32), axis=0)


def solution(mesh):
    placed = (
        P(("grp", "seg"), None),
        P(("grp", "seg")),
        P(),
        P(("grp", "seg"), None),
        P(("grp", "seg"), None),
        P(("grp", "seg")),
    )
    return jax.shard_map(
        on_device, mesh=mesh, in_specs=placed, out_specs=P(("grp", "seg"), None), check_vma=False
    )
```

time: 90 us -> 80.9 us (0.90)
  Pallas kernels: 17.8 us -> 8.95 us
  other arithmetic: 4.65 us -> 1.13 us
  local copies, waits for them, and re-layouts: 1.34 us -> 3.54 us
  waiting for transfers between devices: 0.01 us -> 1.17 us
    pallas_call x1, Pallas kernels: 13.1 us -> 8.04 us  [on_device(): pl.pallas_call(correlate_kernel, out_shape=[jax.ShapeDtypeStruct((pairs,...]
    unnamed x0 -> x16, local copies, waits for them, and re-layouts: none -> 3.54 us
    pallas_call x1, Pallas kernels: 2.77 us -> 0.7 us  [on_device(): pl.pallas_call(own_kernel, out_shape=jax.ShapeDtypeStruct((bins, LAGS), j...]
    pallas_call x1, Pallas kernels: 1.94 us -> 0.2 us  [on_device(): pl.pallas_call(whiten_kernel, out_shape=jax.ShapeDtypeStruct(spectra.shap...]
    convert_element_type x1, other arithmetic: 1.63 us -> 0.27 us  [on_device(): lax.all_gather(white.astype(jnp.float16), 'grp', axis=0, tiled=True)]
    reshape x1 -> x0, local copies, waits for them, and re-layouts: 1.34 us -> none  [on_device(): gap_counts.reshape(stations, 1)]
    convert_element_type x1, other arithmetic: 1.34 us -> 0.11 us  [on_device(): (kept + arrived.astype(jnp.float32)).astype(jnp.bfloat16)]
    ppermute x1, waiting for transfers between devices: 0.01 us -> 1.17 us  [on_device(): arrived = lax.ppermute(away, 'seg', [(i, i ^ 1) for i in range(seg)])]
  transfers between devices with their start and end apart: 1 -> 1, of which waited for: 0 -> 1; matrix products, arithmetic and copies ran while one was open for 0% -> 0% of each run, Pallas kernels for 3% -> 1%
where the time goes in v2:
time: 80.9 us; the launch traced here: 80.4 us
  blocking collectives  63.5 us (78%)
  Pallas kernels  8.95 us (11%)
  local copies, waits for them, and re-layouts  3.54 us (4%)
  starting transfers between devices  1.92 us (2%)
  waiting for transfers between devices  1.17 us (1%)
  other arithmetic  1.13 us (1%)
    all_gather x1, blocking collectives, on_device(): lax.all_gather(white.astype(jnp.float16), 'grp', axis=0, tiled=True)  36.4 us
    all_to_all x1, blocking collectives, on_device(): lax.all_to_all(chip, 'seg', split_axis=0, concat_axis=0, tiled=True, axis...  27.1 us
    pallas_call x1, Pallas kernels, on_device(): pl.pallas_call(correlate_kernel, out_shape=[jax.ShapeDtypeStruct((pairs,...  8.04 us
    unnamed x16, local copies, waits for them, and re-layouts  3.54 us
    ppermute x1, starting transfers between devices, on_device(): arrived = lax.ppermute(away, 'seg', [(i, i ^ 1) for i in range(seg)])  1.92 us
  transfers between devices with their start and end apart: 1, of which 1 were waited for; matrix products, arithmetic and copies ran while one was open for 0% of the time, Pallas kernels for 1%

profile of v2, /device:TPU:6, one launch (start us, length us, event | category | flops | bytes accessed | tf_op | source)
XLA Modules:
  0.0 80.4 jit_solution(17817118149275047406)
XLA Ops:
  0.0 0.0 copy-start.2
  0.0 0.9 %copy-done.2 = bf16[32,4096]{1,0:T(8,128)(2,1)S(1)} copy-done((bf16[32,4096]{1,0:T(8,128)(2,1)S(1)}, bf16[32,4096]{1,0:T(8,128)(2,1)}, u32[]{:S(2)}) %copy-start.2) | copy-done | bytes 262168
  1.0 0.0 copy-start.7
  1.0 0.7 copy-done.7
  1.6 0.2 shard_map.82
  1.9 0.0 copy-start.3
  1.9 0.0 copy-start.4
  1.9 0.0 copy-start.6
  1.9 36.4 %all-gather.1 = f16[256,4096]{1,0:T(8,128)(2,1)S(1)} all-gather(f16[32,4096]{1,0:T(8,128)(2,1)S(1)} %convert_element_type.15), channel_id=1, replica_groups=mesh['grp'=8,'seg'=64] {'grp'}, dimensions={0}, use_global_device_ids=true | all-gather | bytes 2359296 | tf_op jit(solution)/shard_map/all_gather | solution.py:114
  38.3 0.0 copy-start
  38.3 0.0 copy-start.1
  38.3 0.0 copy-start.5
  38.3 0.3 convert_element_type.16.white_ref
  38.6 0.0 copy-done.3
  38.6 0.0 copy-done.4
  38.6 0.0 copy-done.6
  38.6 1.3 %copy-done = f32[256,2048]{1,0:T(8,128)S(1)} copy-done((f32[256,2048]{1,0:T(8,128)S(1)}, f32[256,2048]{1,0:T(8,128)}, u32[]{:S(2)}) %copy-start) | copy-done | bytes 2097176
  39.9 0.6 copy-done.1
  40.6 0.0 copy-done.5
  40.6 8.0 %shard_map.83 = (bf16[1024,256]{1,0:T(8,128)(2,1)S(1)}, bf16[1024,256]{1,0:T(8,128)(2,1)S(1)}) custom-call(s32[2,1024]{1,0:T(2,128)S(1)} %bitcast.6, s32[1,1024]{1,0:T(1,128)S(1)} %bitcast.8, s32[1,1024]{1,0:T(1,128)S(1)} %bitcast.10, bf16[256,4096]{1,0:T(8,128)(2,1)S(1)} %convert_element_type.16.white_ref, f32[1,2048]{1,0:T(1,128)S(1)} %bitcast.7, ...), custom_call_target="tpu_custom_call" | custom-call | tf_op jit(solution)/shard_map/pallas_call | solution.py:119
  48.6 1.9 %collective-permute-start = (bf16[1024,256]{1,0:T(8,128)(2,1)S(1)}, bf16[1024,256]{1,0:T(8,128)(2,1)S(1)}, u32[]{:S(2)}, u32[]{:S(2)}) collective-permute-start(bf16[1024,256]{1,0:T(8,128)(2,1)S(1)} %get-tuple-element.8), channel_id=1, source_target_pairs={{0,1},{1,0},{2,3},{3,2},{4,5},{5,4},{6,7},{7,6},{8,9},{9,8},{10,11... | collective-permute-start | bytes 1572872 | tf_op jit(solution)/shard_map/ppermute | solution.py:135
  50.5 0.7 shard_map.84
  51.2 1.2 %collective-permute-done = bf16[1024,256]{1,0:T(8,128)(2,1)S(1)} collective-permute-done((bf16[1024,256]{1,0:T(8,128)(2,1)S(1)}, bf16[1024,256]{1,0:T(8,128)(2,1)S(1)}, u32[]{:S(2)}, u32[]{:S(2)}) %collective-permute-start) | collective-permute-done | bytes 524320 | tf_op jit(solution)/shard_map/ppermute | solution.py:135
  52.4 0.1 add_convert_fusion
  52.5 27.1 %all_to_all.5 = bf16[32,32,256]{2,1,0:T(8,128)(2,1)S(1)} all-to-all(bf16[32,32,256]{2,1,0:T(8,128)(2,1)S(1)} %bitcast.13), channel_id=1, replica_groups={{0,2,4,6,8,10,12,14,16,18,20,22,24,26,28,30,32,34,36,38,40,42,44,46,48,..., dimensions={0} | all-to-all | bytes 1048576 | tf_op jit(solution)/shard_map/all_to_all | solution.py:143
  79.7 0.7 convert_reduce_fusion
  (1 shorter events, 0.0 us)
Async XLA Ops:
  0.0 0.9 %copy-start.2 = (bf16[32,4096]{1,0:T(8,128)(2,1)S(1)}, bf16[32,4096]{1,0:T(8,128)(2,1)}, u32[]{:S(2)}) copy-start(bf16[32,4096]{1,0:T(8,128)(2,1)} %spectra_ref.1) | copy-start | bytes 786436
  1.0 0.7 copy-start.7
  1.9 36.7 %copy-start.3 = (s32[1024,2]{0,1:T(2,128)S(1)}, s32[1024,2]{0,1:T(2,128)}, u32[]{:S(2)}) copy-start(s32[1024,2]{0,1:T(2,128)} %param.11) | copy-start | bytes 24580
  1.9 36.7 %copy-start.4 = (f32[2048]{0:T(1024)S(1)}, f32[2048]{0:T(1024)}, u32[]{:S(2)}) copy-start(f32[2048]{0:T(1024)} %param.10) | copy-start | bytes 24580
  1.9 36.7 %copy-start.6 = (s32[1024]{0:T(1024)S(1)}, s32[1024]{0:T(1024)}, u32[]{:S(2)}) copy-start(s32[1024]{0:T(1024)} %param.13) | copy-start | bytes 12292
  38.3 1.6 %copy-start = (f32[256,2048]{1,0:T(8,128)S(1)}, f32[256,2048]{1,0:T(8,128)}, u32[]{:S(2)}) copy-start(f32[256,2048]{1,0:T(8,128)} %constant.7.clone.sin_ref) | copy-start | bytes 6291460
  38.3 2.2 %copy-start.1 = (f32[256,2048]{1,0:T(8,128)S(1)}, f32[256,2048]{1,0:T(8,128)}, u32[]{:S(2)}) copy-start(f32[256,2048]{1,0:T(8,128)} %constant.6.clone.cos_ref) | copy-start | bytes 6291460
  38.3 2.2 %copy-start.5 = (s32[1024,1]{0,1:T(1,128)S(1)}, s32[1024,1]{0,1:T(1,128)}, u32[]{:S(2)}) copy-start(s32[1024,1]{0,1:T(1,128)} %param.12) | copy-start | bytes 12292
  48.6 3.8 %collective-permute-start = (bf16[1024,256]{1,0:T(8,128)(2,1)S(1)}, bf16[1024,256]{1,0:T(8,128)(2,1)S(1)}, u32[]{:S(2)}, u32[]{:S(2)}) collective-permute-start(bf16[1024,256]{1,0:T(8,128)(2,1)S(1)} %get-tuple-element.8), channel_id=1, source_target_pairs={{0,1},{1,0},{2,3},{3,2},{4,5},{5,4},{6,7},{7,6},{8,9},{9,8},{10,11... | collective-permute-start | bytes 1572872 | tf_op jit(solution)/shard_map/ppermute | solution.py:135

commit v3 on v2

--- a/solution.py
+++ b/solution.py
@@ -13,6 +13,7 @@
 SAMPLES = 72000
 SLOTS_DEV = 32
 LIFT = 256.0
+FINE = 16
 COLUMNS = 256
 ROWS = 512
 BIN_ROWS = 256
@@ -21,9 +22,10 @@
 
 def tables():
     freqs = np.arange(F, dtype=np.int64)
-    shifts = np.arange(LAGS, dtype=np.int64) - LAGS // 2
-    angles = ((shifts[:, None] * freqs[None, :]) % (2 * F)).astype(np.float64) * (math.pi / F)
-    return np.cos(angles).astype(np.float32), (-np.sin(angles)).astype(np.float32)
+    coarse = np.arange(0, LAGS, FINE, dtype=np.int64) - LAGS // 2
+    fine = np.arange(FINE, dtype=np.int64)
+    angles = [(k[:, None] * freqs[None, :]) % (2 * F) * (math.pi / F) for k in (coarse, fine)]
+    return [f(angle).astype(np.float32) for angle in angles for f in (np.cos, np.sin)]
 
 
 def whiten_kernel(spectra_ref, gap_ref, out_ref):
@@ -56,8 +58,8 @@
 
 
 def correlate_kernel(
-    pairs_ref, owner_ref, slot_ref, white_ref, weight_ref, cos_ref, sin_ref,
-    corr_ref, away_ref, first_ref, second_ref, upper_ref, lower_ref,
+    pairs_ref, owner_ref, slot_ref, white_ref, weight_ref, cos_ref, sin_ref, cos_fine_ref, sin_fine_ref,
+    corr_ref, away_ref, first_ref, second_ref, table_ref,
 ):
     group = white_ref.shape[0]
     pairs = corr_ref.shape[0]
@@ -65,16 +67,22 @@
     first_ref[...] = (ids == pairs_ref[0:1, :]).astype(jnp.float32).T.astype(jnp.bfloat16)
     second_ref[...] = (ids == pairs_ref[1:2, :]).astype(jnp.float32).T.astype(jnp.bfloat16)
     weight = weight_ref[...] * (0.25 / math.sqrt(F) / (LIFT * LIFT))
-    upper_ref[...] = (weight * cos_ref[...]).astype(jnp.bfloat16)
-    lower_ref[...] = (weight * sin_ref[...]).astype(jnp.bfloat16)
+    for lag in range(0, LAGS, FINE):
+        cos = weight * cos_ref[lag // FINE : lag // FINE + 1, :]
+        sin = weight * sin_ref[lag // FINE : lag // FINE + 1, :]
+        upper = (cos * cos_fine_ref[...] - sin * sin_fine_ref[...]).astype(jnp.bfloat16)
+        lower = (-(sin * cos_fine_ref[...] + cos * sin_fine_ref[...])).astype(jnp.bfloat16)
+        for column in range(0, F, COLUMNS):
+            here = slice(column, column + COLUMNS)
+            table_ref[lag : lag + FINE, 2 * column : 2 * column + COLUMNS] = upper[:, here]
+            table_ref[lag : lag + FINE, 2 * column + COLUMNS : 2 * column + 2 * COLUMNS] = lower[:, here]
 
     def pick(one_hot, rows):
         return jnp.dot(one_hot, rows, preferred_element_type=jnp.float32)
 
     def lags(cross, table):
         return lax.dot_general(
-            cross.astype(jnp.bfloat16), table, (((1,), (1,)), ((), ())),
-            preferred_element_type=jnp.float32,
+            cross, table, (((1,), (1,)), ((), ())), preferred_element_type=jnp.float32
         )
 
     for start in range(0, pairs, ROWS):
@@ -87,9 +95,14 @@
             imag = white_ref[:, F + column : F + column + COLUMNS]
             real_one, imag_one = pick(one, real), pick(one, imag)
             real_two, imag_two = pick(two, real), pick(two, imag)
-            total += lags(real_one * real_two + imag_one * imag_two, upper_ref[:, here]) + lags(
-                imag_one * real_two - real_one * imag_two, lower_ref[:, here]
+            cross = jnp.concatenate(
+                [
+                    (real_one * real_two + imag_one * imag_two).astype(jnp.bfloat16),
+                    (imag_one * real_two - real_one * imag_two).astype(jnp.bfloat16),
+                ],
+                axis=1,
             )
+            total += lags(cross, table_ref[:, 2 * column : 2 * column + 2 * COLUMNS])
         corr_ref[rows, :] = total.astype(jnp.bfloat16)
     core = lax.axis_index("seg") & 1
     into_bins(pick_bins(owner_ref, slot_ref, 1 - core), corr_ref, away_ref)
@@ -115,7 +128,6 @@
 
     owner = stack_owner.reshape(1, pairs)
     slot = stack_slot.reshape(1, pairs)
-    cos_table, sin_table = tables()
     corr, away = pl.pallas_call(
         correlate_kernel,
         out_shape=[
@@ -125,12 +137,11 @@
         scratch_shapes=[
             pltpu.VMEM((pairs, group), jnp.bfloat16),
             pltpu.VMEM((pairs, group), jnp.bfloat16),
-            pltpu.VMEM((LAGS, F), jnp.bfloat16),
-            pltpu.VMEM((LAGS, F), jnp.bfloat16),
+            pltpu.VMEM((LAGS, 2 * F), jnp.bfloat16),
         ],
         compiler_params=pltpu.CompilerParams(vmem_limit_bytes=24 * MIB),
     )(
-        pair_list.T, owner, slot, group_rows, band_weight.reshape(1, F), cos_table, sin_table
+        pair_list.T, owner, slot, group_rows, band_weight.reshape(1, F), *tables()
     )
     arrived = lax.ppermute(away, "seg", [(i, i ^ 1) for i in range(seg)])
     kept = pl.pallas_call(

time: 80.9 us -> 79.5 us (0.983)
  local copies, waits for them, and re-layouts: 3.54 us -> 2.38 us
    unnamed x16 -> x20, local copies, waits for them, and re-layouts: 3.54 us -> 2.38 us
where the time goes in v3:
time: 79.5 us; the launch traced here: 78.9 us
  blocking collectives  63.4 us (80%)
  Pallas kernels  8.81 us (11%)
  local copies, waits for them, and re-layouts  2.38 us (3%)
  starting transfers between devices  1.92 us (2%)
  waiting for transfers between devices  1.17 us (1%)
  other arithmetic  1.13 us (1%)
    all_gather x1, blocking collectives, on_device(): lax.all_gather(white.astype(jnp.float16), 'grp', axis=0, tiled=True)  36.3 us
    all_to_all x1, blocking collectives, on_device(): lax.all_to_all(chip, 'seg', split_axis=0, concat_axis=0, tiled=True, axis...  27.1 us
    pallas_call x1, Pallas kernels, on_device(): pl.pallas_call(correlate_kernel, out_shape=[jax.ShapeDtypeStruct((pairs,...  7.91 us
    unnamed x20, local copies, waits for them, and re-layouts  2.38 us
    ppermute x1, starting transfers between devices, on_device(): arrived = lax.ppermute(away, 'seg', [(i, i ^ 1) for i in range(seg)])  1.92 us
  transfers between devices with their start and end apart: 1, of which 1 were waited for; matrix products, arithmetic and copies ran while one was open for 0% of the time, Pallas kernels for 1%

profile of v3, /device:TPU:6, one launch (start us, length us, event | category | flops | bytes accessed | tf_op | source)
XLA Modules:
  0.0 78.9 jit_solution(17877488540667772982)
XLA Ops:
  0.0 0.0 copy-start
  0.0 0.9 %copy-done = bf16[32,4096]{1,0:T(8,128)(2,1)S(1)} copy-done((bf16[32,4096]{1,0:T(8,128)(2,1)S(1)}, bf16[32,4096]{1,0:T(8,128)(2,1)}, u32[]{:S(2)}) %copy-start) | copy-done | bytes 262168
  1.0 0.0 copy-start.9
  1.0 0.7 copy-done.9
  1.6 0.2 shard_map.100
  1.9 36.3 %all-gather.1 = f16[256,4096]{1,0:T(8,128)(2,1)S(1)} all-gather(f16[32,4096]{1,0:T(8,128)(2,1)S(1)} %convert_element_type.15), channel_id=1, replica_groups=mesh['grp'=8,'seg'=64] {'grp'}, dimensions={0}, use_global_device_ids=true | all-gather | bytes 2359296 | tf_op jit(solution)/shard_map/all_gather | solution.py:127
  38.2 0.0 copy-start.1
  38.2 0.0 copy-start.2
  38.2 0.0 copy-start.3
  38.2 0.0 copy-start.4
  38.2 0.0 copy-start.5
  38.2 0.0 copy-start.6
  38.2 0.0 copy-start.7
  38.2 0.0 copy-start.8
  38.2 0.3 convert_element_type.16.white_ref
  38.5 0.6 copy-done.1
  39.1 0.1 copy-done.2
  39.1 0.1 copy-done.3
  39.2 0.1 copy-done.4
  39.3 0.0 copy-done.5
  39.3 0.0 copy-done.6
  39.3 0.0 copy-done.7
  39.3 0.0 copy-done.8
  39.3 7.9 %shard_map.101 = (bf16[1024,256]{1,0:T(8,128)(2,1)S(1)}, bf16[1024,256]{1,0:T(8,128)(2,1)S(1)}) custom-call(s32[2,1024]{1,0:T(2,128)S(1)} %bitcast.6, s32[1,1024]{1,0:T(1,128)S(1)} %bitcast.8, s32[1,1024]{1,0:T(1,128)S(1)} %bitcast.10, bf16[256,4096]{1,0:T(8,128)(2,1)S(1)} %convert_element_type.16.white_ref, f32[1,2048]{1,0:T(1,128)S(1)} %bitcast.7, ...), custom_call_target="tpu_custom_call" | custom-call | tf_op jit(solution)/shard_map/pallas_call | solution.py:131
  47.2 1.9 %collective-permute-start = (bf16[1024,256]{1,0:T(8,128)(2,1)S(1)}, bf16[1024,256]{1,0:T(8,128)(2,1)S(1)}, u32[]{:S(2)}, u32[]{:S(2)}) collective-permute-start(bf16[1024,256]{1,0:T(8,128)(2,1)S(1)} %get-tuple-element.8), channel_id=1, source_target_pairs={{0,1},{1,0},{2,3},{3,2},{4,5},{5,4},{6,7},{7,6},{8,9},{9,8},{10,11... | collective-permute-start | bytes 1572872 | tf_op jit(solution)/shard_map/ppermute | solution.py:146
  49.1 0.7 shard_map.102
  49.8 1.2 %collective-permute-done = bf16[1024,256]{1,0:T(8,128)(2,1)S(1)} collective-permute-done((bf16[1024,256]{1,0:T(8,128)(2,1)S(1)}, bf16[1024,256]{1,0:T(8,128)(2,1)S(1)}, u32[]{:S(2)}, u32[]{:S(2)}) %collective-permute-start) | collective-permute-done | bytes 524320 | tf_op jit(solution)/shard_map/ppermute | solution.py:146
  51.0 0.1 add_convert_fusion
  51.1 27.1 %all_to_all.5 = bf16[32,32,256]{2,1,0:T(8,128)(2,1)S(1)} all-to-all(bf16[32,32,256]{2,1,0:T(8,128)(2,1)S(1)} %bitcast.13), channel_id=1, replica_groups={{0,2,4,6,8,10,12,14,16,18,20,22,24,26,28,30,32,34,36,38,40,42,44,46,48,..., dimensions={0} | all-to-all | bytes 1048576 | tf_op jit(solution)/shard_map/all_to_all | solution.py:154
  78.2 0.7 convert_reduce_fusion
  (1 shorter events, 0.0 us)
Async XLA Ops:
  0.0 0.9 %copy-start = (bf16[32,4096]{1,0:T(8,128)(2,1)S(1)}, bf16[32,4096]{1,0:T(8,128)(2,1)}, u32[]{:S(2)}) copy-start(bf16[32,4096]{1,0:T(8,128)(2,1)} %spectra_ref.1) | copy-start | bytes 786436
  1.0 0.7 copy-start.9
  38.2 0.9 %copy-start.1 = (f32[16,2048]{1,0:T(8,128)S(1)}, f32[16,2048]{1,0:T(8,128)}, u32[]{:S(2)}) copy-start(f32[16,2048]{1,0:T(8,128)} %constant.13.clone.sin_fine_ref) | copy-start | bytes 393220
  38.2 1.0 %copy-start.2 = (f32[16,2048]{1,0:T(8,128)S(1)}, f32[16,2048]{1,0:T(8,128)}, u32[]{:S(2)}) copy-start(f32[16,2048]{1,0:T(8,128)} %constant.12.clone.cos_fine_ref) | copy-start | bytes 393220
  38.2 1.0 %copy-start.3 = (f32[16,2048]{1,0:T(8,128)S(1)}, f32[16,2048]{1,0:T(8,128)}, u32[]{:S(2)}) copy-start(f32[16,2048]{1,0:T(8,128)} %constant.11.clone.sin_ref) | copy-start | bytes 393220
  38.2 1.1 %copy-start.4 = (f32[16,2048]{1,0:T(8,128)S(1)}, f32[16,2048]{1,0:T(8,128)}, u32[]{:S(2)}) copy-start(f32[16,2048]{1,0:T(8,128)} %constant.10.clone.cos_ref) | copy-start | bytes 393220
  38.2 1.1 %copy-start.5 = (s32[1024,2]{0,1:T(2,128)S(1)}, s32[1024,2]{0,1:T(2,128)}, u32[]{:S(2)}) copy-start(s32[1024,2]{0,1:T(2,128)} %param.13) | copy-start | bytes 24580
  38.2 1.1 %copy-start.6 = (f32[2048]{0:T(1024)S(1)}, f32[2048]{0:T(1024)}, u32[]{:S(2)}) copy-start(f32[2048]{0:T(1024)} %param.12) | copy-start | bytes 24580
  38.2 1.1 %copy-start.7 = (s32[1024,1]{0,1:T(1,128)S(1)}, s32[1024,1]{0,1:T(1,128)}, u32[]{:S(2)}) copy-start(s32[1024,1]{0,1:T(1,128)} %param.14) | copy-start | bytes 12292
  38.2 1.1 %copy-start.8 = (s32[1024]{0:T(1024)S(1)}, s32[1024]{0:T(1024)}, u32[]{:S(2)}) copy-start(s32[1024]{0:T(1024)} %param.15) | copy-start | bytes 12292
  47.2 3.8 %collective-permute-start = (bf16[1024,256]{1,0:T(8,128)(2,1)S(1)}, bf16[1024,256]{1,0:T(8,128)(2,1)S(1)}, u32[]{:S(2)}, u32[]{:S(2)}) collective-permute-start(bf16[1024,256]{1,0:T(8,128)(2,1)S(1)} %get-tuple-element.8), channel_id=1, source_target_pairs={{0,1},{1,0},{2,3},{3,2},{4,5},{5,4},{6,7},{7,6},{8,9},{9,8},{10,11... | collective-permute-start | bytes 1572872 | tf_op jit(solution)/shard_map/ppermute | solution.py:146

commit v4 on v3

--- a/solution.py
+++ b/solution.py
@@ -28,16 +28,11 @@
     return [f(angle).astype(np.float32) for angle in angles for f in (np.cos, np.sin)]
 
 
-def whiten_kernel(spectra_ref, gap_ref, out_ref):
-    stations = spectra_ref.shape[0]
-    values = spectra_ref[...].astype(jnp.float32)
-    power = jnp.mean(values * values, axis=1, keepdims=True)
-    kept = jnp.broadcast_to(SAMPLES - gap_ref[...].astype(jnp.float32), (stations, stations))
-    here = lax.broadcasted_iota(jnp.int32, (stations, stations), 0)
-    along = lax.broadcasted_iota(jnp.int32, (stations, stations), 1)
-    kept = jnp.sum(jnp.where(here == along, kept, 0.0), axis=1, keepdims=True)
-    factor = jnp.sqrt(SAMPLES / kept) / jnp.sqrt(power + 1e-06)
-    out_ref[...] = (values * factor).astype(jnp.bfloat16) * LIFT
+def whiten(spectra, gap_counts):
+    values = spectra.astype(jnp.float32)
+    power = jnp.mean(values * values, axis=1)
+    factor = jnp.sqrt(SAMPLES / (SAMPLES - gap_counts.astype(jnp.float32))) / jnp.sqrt(power + 1e-06)
+    return (values * factor[:, None]).astype(jnp.bfloat16)
 
 
 def pick_bins(owner_ref, slot_ref, parity):
@@ -119,12 +114,8 @@
     seg = lax.axis_size("seg")
     group = stations * lax.axis_size("grp")
     bins = seg // 2 * SLOTS_DEV
-    white = pl.pallas_call(
-        whiten_kernel,
-        out_shape=jax.ShapeDtypeStruct(spectra.shape, jnp.bfloat16),
-        compiler_params=pltpu.CompilerParams(vmem_limit_bytes=8 * MIB),
-    )(spectra, gap_counts.reshape(1, stations))
-    group_rows = lax.all_gather(white.astype(jnp.float16), "grp", axis=0, tiled=True).astype(jnp.bfloat16)
+    lifted = (whiten(spectra, gap_counts) * LIFT).astype(jnp.float16)
+    group_rows = lax.all_gather(lifted, "grp", axis=0, tiled=True).astype(jnp.bfloat16)
 
     owner = stack_owner.reshape(1, pairs)
     slot = stack_slot.reshape(1, pairs)

time: 79.5 us -> 80.5 us (1.013)
  other arithmetic: 1.13 us -> 3.97 us
  local copies, waits for them, and re-layouts: 2.38 us -> 0.78 us
    unnamed x20 -> x16, local copies, waits for them, and re-layouts: 2.38 us -> 0.78 us
    reduce_sum x0 -> x1, other arithmetic: none -> 1.11 us  [whiten(): power = jnp.mean(values * values, axis=1)]
    convert_element_type x2, other arithmetic: 0.32 us -> 1.38 us  [the longest x1 1.1 us: on_device(): lifted = (whiten(spectra, gap_counts) * LIFT).astype(jnp.float16)]
where the time goes in v4:
time: 80.5 us; the launch traced here: 79.9 us
  blocking collectives  63.4 us (79%)
  Pallas kernels  8.61 us (11%)
  other arithmetic  3.97 us (5%)
  starting transfers between devices  1.92 us (2%)
  waiting for transfers between devices  1.17 us (1%)
    all_gather x1, blocking collectives, on_device(): lax.all_gather(lifted, 'grp', axis=0, tiled=True).astype(jnp.bfloat16)  36.3 us
    all_to_all x1, blocking collectives, on_device(): lax.all_to_all(chip, 'seg', split_axis=0, concat_axis=0, tiled=True, axis...  27.1 us
    pallas_call x1, Pallas kernels, on_device(): pl.pallas_call(correlate_kernel, out_shape=[jax.ShapeDtypeStruct((pairs,...  7.91 us
    ppermute x1, starting transfers between devices, on_device(): arrived = lax.ppermute(away, 'seg', [(i, i ^ 1) for i in range(seg)])  1.92 us
  transfers between devices with their start and end apart: 1, of which 1 were waited for; matrix products, arithmetic and copies ran while one was open for 0% of the time, Pallas kernels for 1%

profile of v4, /device:TPU:6, one launch (start us, length us, event | category | flops | bytes accessed | tf_op | source)
XLA Modules:
  0.0 79.9 jit_solution(10173254845362260888)
XLA Ops:
  0.0 1.1 %fusion = f32[32]{0:T(128)S(1)} fusion(bf16[32,4096]{1,0:T(8,128)(2,1)} %param.10), kind=kLoop, calls=%fused_computation.4 | loop fusion | flops 393184 | bytes 262272 | tf_op jit(solution)/shard_map/reduce_sum | solution.py:33
  1.1 0.7 rsqrt_multiply_fusion
  1.8 1.1 %fusion.3 = f16[32,4096]{1,0:T(8,128)(2,1)S(1)} fusion(bf16[32,4096]{1,0:T(8,128)(2,1)} %param.10, f32[32]{0:T(128)S(1)} %rsqrt_multiply_fusion), kind=kLoop, calls=%fused_computation.7 | loop fusion | flops 655360 | bytes 524416 | tf_op jit(solution)/shard_map/convert_element_type | solution.py:117
  2.9 36.3 %all-gather.1 = f16[256,4096]{1,0:T(8,128)(2,1)S(1)} all-gather(f16[32,4096]{1,0:T(8,128)(2,1)S(1)} %fusion.3), channel_id=1, replica_groups=mesh['grp'=8,'seg'=64] {'grp'}, dimensions={0}, use_global_device_ids=true | all-gather | bytes 2359296 | tf_op jit(solution)/shard_map/all_gather | solution.py:118
  39.2 0.0 copy-start
  39.2 0.0 copy-start.1
  39.2 0.0 copy-start.2
  39.2 0.0 copy-start.3
  39.2 0.0 copy-start.4
  39.2 0.0 copy-start.5
  39.2 0.0 copy-start.6
  39.2 0.0 copy-start.7
  39.2 0.3 convert_element_type.28.white_ref
  39.5 0.6 copy-done
  40.1 0.1 copy-done.1
  40.1 0.1 copy-done.2
  40.2 0.1 copy-done.3
  40.3 0.0 copy-done.4
  40.3 0.0 copy-done.5
  40.3 0.0 copy-done.6
  40.3 0.0 copy-done.7
  40.3 7.9 %shard_map.100 = (bf16[1024,256]{1,0:T(8,128)(2,1)S(1)}, bf16[1024,256]{1,0:T(8,128)(2,1)S(1)}) custom-call(s32[2,1024]{1,0:T(2,128)S(1)} %bitcast.5, s32[1,1024]{1,0:T(1,128)S(1)} %bitcast.7, s32[1,1024]{1,0:T(1,128)S(1)} %bitcast.9, bf16[256,4096]{1,0:T(8,128)(2,1)S(1)} %convert_element_type.28.white_ref, f32[1,2048]{1,0:T(1,128)S(1)} %bitcast.6, ...), custom_call_target="tpu_custom_call" | custom-call | tf_op jit(solution)/shard_map/pallas_call | solution.py:122
  48.2 1.9 %collective-permute-start = (bf16[1024,256]{1,0:T(8,128)(2,1)S(1)}, bf16[1024,256]{1,0:T(8,128)(2,1)S(1)}, u32[]{:S(2)}, u32[]{:S(2)}) collective-permute-start(bf16[1024,256]{1,0:T(8,128)(2,1)S(1)} %get-tuple-element.8), channel_id=1, source_target_pairs={{0,1},{1,0},{2,3},{3,2},{4,5},{5,4},{6,7},{7,6},{8,9},{9,8},{10,11... | collective-permute-start | bytes 1572872 | tf_op jit(solution)/shard_map/ppermute | solution.py:137
  50.1 0.7 shard_map.101
  50.8 1.2 %collective-permute-done = bf16[1024,256]{1,0:T(8,128)(2,1)S(1)} collective-permute-done((bf16[1024,256]{1,0:T(8,128)(2,1)S(1)}, bf16[1024,256]{1,0:T(8,128)(2,1)S(1)}, u32[]{:S(2)}, u32[]{:S(2)}) %collective-permute-start) | collective-permute-done | bytes 524320 | tf_op jit(solution)/shard_map/ppermute | solution.py:137
  52.0 0.1 add_convert_fusion
  52.1 27.1 %all_to_all.5 = bf16[32,32,256]{2,1,0:T(8,128)(2,1)S(1)} all-to-all(bf16[32,32,256]{2,1,0:T(8,128)(2,1)S(1)} %bitcast.11), channel_id=1, replica_groups={{0,2,4,6,8,10,12,14,16,18,20,22,24,26,28,30,32,34,36,38,40,42,44,46,48,..., dimensions={0} | all-to-all | bytes 1048576 | tf_op jit(solution)/shard_map/all_to_all | solution.py:145
  79.3 0.7 convert_reduce_fusion
Async XLA Ops:
  39.2 0.9 %copy-start = (f32[16,2048]{1,0:T(8,128)S(1)}, f32[16,2048]{1,0:T(8,128)}, u32[]{:S(2)}) copy-start(f32[16,2048]{1,0:T(8,128)} %constant.22.clone.sin_fine_ref) | copy-start | bytes 393220
  39.2 1.0 %copy-start.1 = (f32[16,2048]{1,0:T(8,128)S(1)}, f32[16,2048]{1,0:T(8,128)}, u32[]{:S(2)}) copy-start(f32[16,2048]{1,0:T(8,128)} %constant.21.clone.cos_fine_ref) | copy-start | bytes 393220
  39.2 1.0 %copy-start.2 = (f32[16,2048]{1,0:T(8,128)S(1)}, f32[16,2048]{1,0:T(8,128)}, u32[]{:S(2)}) copy-start(f32[16,2048]{1,0:T(8,128)} %constant.20.clone.sin_ref) | copy-start | bytes 393220
  39.2 1.1 %copy-start.3 = (f32[16,2048]{1,0:T(8,128)S(1)}, f32[16,2048]{1,0:T(8,128)}, u32[]{:S(2)}) copy-start(f32[16,2048]{1,0:T(8,128)} %constant.19.clone.cos_ref) | copy-start | bytes 393220
  39.2 1.1 %copy-start.4 = (s32[1024,2]{0,1:T(2,128)S(1)}, s32[1024,2]{0,1:T(2,128)}, u32[]{:S(2)}) copy-start(s32[1024,2]{0,1:T(2,128)} %param.13) | copy-start | bytes 24580
  39.2 1.1 %copy-start.5 = (f32[2048]{0:T(1024)S(1)}, f32[2048]{0:T(1024)}, u32[]{:S(2)}) copy-start(f32[2048]{0:T(1024)} %param.12) | copy-start | bytes 24580
  39.2 1.1 %copy-start.6 = (s32[1024,1]{0,1:T(1,128)S(1)}, s32[1024,1]{0,1:T(1,128)}, u32[]{:S(2)}) copy-start(s32[1024,1]{0,1:T(1,128)} %param.14) | copy-start | bytes 12292
  39.2 1.1 %copy-start.7 = (s32[1024]{0:T(1024)S(1)}, s32[1024]{0:T(1024)}, u32[]{:S(2)}) copy-start(s32[1024]{0:T(1024)} %param.15) | copy-start | bytes 12292
  48.2 3.8 %collective-permute-start = (bf16[1024,256]{1,0:T(8,128)(2,1)S(1)}, bf16[1024,256]{1,0:T(8,128)(2,1)S(1)}, u32[]{:S(2)}, u32[]{:S(2)}) collective-permute-start(bf16[1024,256]{1,0:T(8,128)(2,1)S(1)} %get-tuple-element.8), channel_id=1, source_target_pairs={{0,1},{1,0},{2,3},{3,2},{4,5},{5,4},{6,7},{7,6},{8,9},{9,8},{10,11... | collective-permute-start | bytes 1572872 | tf_op jit(solution)/shard_map/ppermute | solution.py:137

commit v5 on v3

--- a/solution.py
+++ b/solution.py
@@ -12,6 +12,7 @@
 LAGS = 256
 SAMPLES = 72000
 SLOTS_DEV = 32
+CHIPS_Y, CHIPS_X = 8, 4
 LIFT = 256.0
 FINE = 16
 COLUMNS = 256
@@ -42,7 +43,8 @@
 
 def pick_bins(owner_ref, slot_ref, parity):
     owner = owner_ref[...]
-    local = (owner >> 1) * SLOTS_DEV + slot_ref[...]
+    chip = owner >> 1
+    local = ((chip % CHIPS_X) * CHIPS_Y + chip // CHIPS_X) * SLOTS_DEV + slot_ref[...]
     return jnp.where((owner & 1) == parity, local, -1)
 
 
@@ -150,10 +152,20 @@
         compiler_params=pltpu.CompilerParams(vmem_limit_bytes=8 * MIB),
         cost_estimate=pl.CostEstimate(flops=2 * bins * pairs * LAGS, bytes_accessed=2 << 20, transcendentals=0),
     )(owner, slot, corr)
-    chip = (kept + arrived.astype(jnp.float32)).astype(jnp.bfloat16).reshape(seg // 2, SLOTS_DEV, LAGS)
+    chip = (kept + arrived.astype(jnp.float32)).astype(jnp.bfloat16)
+    rows = chip.reshape(CHIPS_X, CHIPS_Y * SLOTS_DEV, LAGS)
     got = lax.all_to_all(
-        chip, "seg", split_axis=0, concat_axis=0, tiled=True,
-        axis_index_groups=[list(range(core, seg, 2)) for core in range(2)],
+        rows, "seg", split_axis=0, concat_axis=0, tiled=True,
+        axis_index_groups=[
+            [(y * CHIPS_X + x) * 2 + core for x in range(CHIPS_X)] for y in range(CHIPS_Y) for core in range(2)
+        ],
+    )
+    rows = jnp.sum(got.astype(jnp.float32), axis=0).astype(jnp.bfloat16).reshape(CHIPS_Y, SLOTS_DEV, LAGS)
+    got = lax.all_to_all(
+        rows, "seg", split_axis=0, concat_axis=0, tiled=True,
+        axis_index_groups=[
+            [(y * CHIPS_X + x) * 2 + core for y in range(CHIPS_Y)] for x in range(CHIPS_X) for core in range(2)
+        ],
     )
     return jnp.sum(got.astype(jnp.float32), axis=0)
 

time: 79.5 us -> 81 us (1.019)
  blocking collectives: 63.4 us -> 64.6 us
    all_to_all x1 -> x2, blocking collectives: 27.1 us -> 28.3 us  [on_device(): lax.all_to_all(rows, 'seg', split_axis=0, concat_axis=0, tiled=True, axis...]
where the time goes in v5:
time: 81 us; the launch traced here: 80.1 us
  blocking collectives  64.6 us (80%)
  Pallas kernels  8.82 us (11%)
  local copies, waits for them, and re-layouts  2.38 us (3%)
  starting transfers between devices  1.92 us (2%)
  waiting for transfers between devices  1.17 us (1%)
  other arithmetic  1.15 us (1%)
    all_gather x1, blocking collectives, on_device(): lax.all_gather(white.astype(jnp.float16), 'grp', axis=0, tiled=True)  36.3 us
    all_to_all x2, blocking collectives, on_device(): lax.all_to_all(rows, 'seg', split_axis=0, concat_axis=0, tiled=True, axis...  28.3 us
    pallas_call x1, Pallas kernels, on_device(): pl.pallas_call(correlate_kernel, out_shape=[jax.ShapeDtypeStruct((pairs,...  7.91 us
    unnamed x20, local copies, waits for them, and re-layouts  2.38 us
    ppermute x1, starting transfers between devices, on_device(): arrived = lax.ppermute(away, 'seg', [(i, i ^ 1) for i in range(seg)])  1.92 us
  transfers between devices with their start and end apart: 1, of which 1 were waited for; matrix products, arithmetic and copies ran while one was open for 0% of the time, Pallas kernels for 1%

profile of v5, /device:TPU:6, one launch (start us, length us, event | category | flops | bytes accessed | tf_op | source)
XLA Modules:
  0.0 80.1 jit_solution(857291598280372371)
XLA Ops:
  0.0 0.0 copy-start
  0.0 0.9 %copy-done = bf16[32,4096]{1,0:T(8,128)(2,1)S(1)} copy-done((bf16[32,4096]{1,0:T(8,128)(2,1)S(1)}, bf16[32,4096]{1,0:T(8,128)(2,1)}, u32[]{:S(2)}) %copy-start) | copy-done | bytes 262168
  1.0 0.0 copy-start.9
  1.0 0.7 copy-done.9
  1.6 0.2 shard_map.100
  1.9 36.3 %all-gather.1 = f16[256,4096]{1,0:T(8,128)(2,1)S(1)} all-gather(f16[32,4096]{1,0:T(8,128)(2,1)S(1)} %convert_element_type.17), channel_id=1, replica_groups=mesh['grp'=8,'seg'=64] {'grp'}, dimensions={0}, use_global_device_ids=true | all-gather | bytes 2359296 | tf_op jit(solution)/shard_map/all_gather | solution.py:129
  38.2 0.0 copy-start.1
  38.2 0.0 copy-start.2
  38.2 0.0 copy-start.3
  38.2 0.0 copy-start.4
  38.2 0.0 copy-start.5
  38.2 0.0 copy-start.6
  38.2 0.0 copy-start.7
  38.2 0.0 copy-start.8
  38.2 0.3 convert_element_type.18.white_ref
  38.5 0.6 copy-done.1
  39.1 0.1 copy-done.2
  39.1 0.1 copy-done.3
  39.2 0.1 copy-done.4
  39.3 0.0 copy-done.5
  39.3 0.0 copy-done.6
  39.3 0.0 copy-done.7
  39.3 0.0 copy-done.8
  39.3 7.9 %shard_map.101 = (bf16[1024,256]{1,0:T(8,128)(2,1)S(1)}, bf16[1024,256]{1,0:T(8,128)(2,1)S(1)}) custom-call(s32[2,1024]{1,0:T(2,128)S(1)} %bitcast.7, s32[1,1024]{1,0:T(1,128)S(1)} %bitcast.9, s32[1,1024]{1,0:T(1,128)S(1)} %bitcast.11, bf16[256,4096]{1,0:T(8,128)(2,1)S(1)} %convert_element_type.18.white_ref, f32[1,2048]{1,0:T(1,128)S(1)} %bitcast.8, ...), custom_call_target="tpu_custom_call" | custom-call | tf_op jit(solution)/shard_map/pallas_call | solution.py:133
  47.2 1.9 %collective-permute-start = (bf16[1024,256]{1,0:T(8,128)(2,1)S(1)}, bf16[1024,256]{1,0:T(8,128)(2,1)S(1)}, u32[]{:S(2)}, u32[]{:S(2)}) collective-permute-start(bf16[1024,256]{1,0:T(8,128)(2,1)S(1)} %get-tuple-element.8), channel_id=1, source_target_pairs={{0,1},{1,0},{2,3},{3,2},{4,5},{5,4},{6,7},{7,6},{8,9},{9,8},{10,11... | collective-permute-start | bytes 1572872 | tf_op jit(solution)/shard_map/ppermute | solution.py:148
  49.1 0.7 shard_map.102
  49.8 1.2 %collective-permute-done = bf16[1024,256]{1,0:T(8,128)(2,1)S(1)} collective-permute-done((bf16[1024,256]{1,0:T(8,128)(2,1)S(1)}, bf16[1024,256]{1,0:T(8,128)(2,1)S(1)}, u32[]{:S(2)}, u32[]{:S(2)}) %collective-permute-start) | collective-permute-done | bytes 524320 | tf_op jit(solution)/shard_map/ppermute | solution.py:148
  51.0 0.1 add_convert_fusion
  51.1 12.3 %all_to_all.10 = bf16[4,256,256]{2,1,0:T(8,128)(2,1)S(1)} all-to-all(bf16[4,256,256]{2,1,0:T(8,128)(2,1)S(1)} %bitcast.14), channel_id=1, replica_groups={{0,2,4,6},{1,3,5,7},{8,10,12,14},{9,11,13,15},{16,18,20,22},{17,19,21,2..., dimensions={0} | all-to-all | bytes 1048576 | tf_op jit(solution)/shard_map/all_to_all | solution.py:157
  63.4 0.1 reduce_sum.21
  63.5 16.0 %all_to_all.11 = bf16[8,32,256]{2,1,0:T(8,128)(2,1)S(1)} all-to-all(bf16[8,32,256]{2,1,0:T(8,128)(2,1)S(1)} %bitcast.15), channel_id=1, replica_groups={{0,8,16,24,32,40,48,56},{1,9,17,25,33,41,49,57},{2,10,18,26,34,42,50,58..., dimensions={0} | all-to-all | bytes 262144 | tf_op jit(solution)/shard_map/all_to_all | solution.py:164
  79.5 0.6 convert_reduce_fusion
  (1 shorter events, 0.0 us)
Async XLA Ops:
  0.0 0.9 %copy-start = (bf16[32,4096]{1,0:T(8,128)(2,1)S(1)}, bf16[32,4096]{1,0:T(8,128)(2,1)}, u32[]{:S(2)}) copy-start(bf16[32,4096]{1,0:T(8,128)(2,1)} %spectra_ref.1) | copy-start | bytes 786436
  1.0 0.7 copy-start.9
  38.2 0.9 %copy-start.1 = (f32[16,2048]{1,0:T(8,128)S(1)}, f32[16,2048]{1,0:T(8,128)}, u32[]{:S(2)}) copy-start(f32[16,2048]{1,0:T(8,128)} %constant.15.clone.sin_fine_ref) | copy-start | bytes 393220
  38.2 1.0 %copy-start.2 = (f32[16,2048]{1,0:T(8,128)S(1)}, f32[16,2048]{1,0:T(8,128)}, u32[]{:S(2)}) copy-start(f32[16,2048]{1,0:T(8,128)} %constant.14.clone.cos_fine_ref) | copy-start | bytes 393220
  38.2 1.0 %copy-start.3 = (f32[16,2048]{1,0:T(8,128)S(1)}, f32[16,2048]{1,0:T(8,128)}, u32[]{:S(2)}) copy-start(f32[16,2048]{1,0:T(8,128)} %constant.13.clone.sin_ref) | copy-start | bytes 393220
  38.2 1.1 %copy-start.4 = (f32[16,2048]{1,0:T(8,128)S(1)}, f32[16,2048]{1,0:T(8,128)}, u32[]{:S(2)}) copy-start(f32[16,2048]{1,0:T(8,128)} %constant.12.clone.cos_ref) | copy-start | bytes 393220
  38.2 1.1 %copy-start.5 = (s32[1024,2]{0,1:T(2,128)S(1)}, s32[1024,2]{0,1:T(2,128)}, u32[]{:S(2)}) copy-start(s32[1024,2]{0,1:T(2,128)} %param.13) | copy-start | bytes 24580
  38.2 1.1 %copy-start.6 = (f32[2048]{0:T(1024)S(1)}, f32[2048]{0:T(1024)}, u32[]{:S(2)}) copy-start(f32[2048]{0:T(1024)} %param.12) | copy-start | bytes 24580
  38.2 1.1 %copy-start.7 = (s32[1024,1]{0,1:T(1,128)S(1)}, s32[1024,1]{0,1:T(1,128)}, u32[]{:S(2)}) copy-start(s32[1024,1]{0,1:T(1,128)} %param.14) | copy-start | bytes 12292
  38.2 1.1 %copy-start.8 = (s32[1024]{0:T(1024)S(1)}, s32[1024]{0:T(1024)}, u32[]{:S(2)}) copy-start(s32[1024]{0:T(1024)} %param.15) | copy-start | bytes 12292
  47.2 3.8 %collective-permute-start = (bf16[1024,256]{1,0:T(8,128)(2,1)S(1)}, bf16[1024,256]{1,0:T(8,128)(2,1)S(1)}, u32[]{:S(2)}, u32[]{:S(2)}) collective-permute-start(bf16[1024,256]{1,0:T(8,128)(2,1)S(1)} %get-tuple-element.8), channel_id=1, source_target_pairs={{0,1},{1,0},{2,3},{3,2},{4,5},{5,4},{6,7},{7,6},{8,9},{9,8},{10,11... | collective-permute-start | bytes 1572872 | tf_op jit(solution)/shard_map/ppermute | solution.py:148

commit v6 on v3

v6 whole, which is shorter than its diff:
```python
import math

import jax
import jax.numpy as jnp
import numpy as np
from jax import lax
from jax.experimental import pallas as pl
from jax.experimental.pallas import tpu as pltpu
from jax.sharding import PartitionSpec as P

F = 2048
LAGS = 256
SAMPLES = 72000
SLOTS_DEV = 32
LIFT = 256.0
FINE = 16
COLUMNS = 256
ROWS = 512
BIN_ROWS = 256
MIB = 1024 * 1024


def tables():
    freqs = np.arange(F, dtype=np.int64)
    coarse = np.arange(0, LAGS, FINE, dtype=np.int64) - LAGS // 2
    fine = np.arange(FINE, dtype=np.int64)
    angles = [(k[:, None] * freqs[None, :]) % (2 * F) * (math.pi / F) for k in (coarse, fine)]
    return [np.concatenate([np.cos(angle), np.sin(angle)]).astype(np.float32) for angle in angles]


def prepare_kernel(
    spectra_hbm, gap_hbm, pairs_hbm, owner_hbm, slot_hbm, weight_hbm, coarse_hbm, fine_hbm,
    white_ref, first_ref, second_ref, bins_ref, table_ref,
    spectra_ref, gap_ref, pairs_ref, owner_ref, slot_ref, weight_ref, coarse_ref, fine_ref, sems,
):
    moved = (
        (weight_hbm, weight_ref), (coarse_hbm, coarse_ref), (fine_hbm, fine_ref), (pairs_hbm, pairs_ref),
        (owner_hbm, owner_ref), (slot_hbm, slot_ref), (gap_hbm, gap_ref), (spectra_hbm, spectra_ref),
    )
    copies = [pltpu.make_async_copy(src, dst, sems.at[i]) for i, (src, dst) in enumerate(moved)]
    for copy in copies:
        copy.start()
    for copy in copies:
        copy.wait()

    weight = weight_ref[...] * (0.25 / math.sqrt(F) / (LIFT * LIFT))
    cos_fine, sin_fine = fine_ref[:FINE, :], fine_ref[FINE:, :]
    count = LAGS // FINE
    for block in range(count):
        cos = weight * coarse_ref[block : block + 1, :]
        sin = weight * coarse_ref[count + block : count + block + 1, :]
        upper = (cos * cos_fine - sin * sin_fine).astype(jnp.bfloat16)
        lower = (-(sin * cos_fine + cos * sin_fine)).astype(jnp.bfloat16)
        rows = slice(block * FINE, block * FINE + FINE)
        for column in range(0, F, COLUMNS):
            here = slice(column, column + COLUMNS)
            table_ref[rows, 2 * column : 2 * column + COLUMNS] = upper[:, here]
            table_ref[rows, 2 * column + COLUMNS : 2 * column + 2 * COLUMNS] = lower[:, here]

    pairs, group = first_ref.shape
    ids = lax.broadcasted_iota(jnp.int32, (group, pairs), 0)
    first_ref[...] = (ids == pairs_ref[0:1, :]).astype(jnp.float32).T.astype(jnp.bfloat16)
    second_ref[...] = (ids == pairs_ref[1:2, :]).astype(jnp.float32).T.astype(jnp.bfloat16)

    core = lax.axis_index("seg") & 1
    owner = owner_ref[...]
    local = (owner >> 1) * SLOTS_DEV + slot_ref[...]
    bins_ref[0:1, :] = jnp.where((owner & 1) == core, -1, local)
    bins_ref[1:2, :] = jnp.where((owner & 1) == core, local, -1)

    stations = spectra_ref.shape[0]
    values = spectra_ref[...].astype(jnp.float32)
    power = jnp.mean(values * values, axis=1, keepdims=True)
    kept = jnp.broadcast_to(SAMPLES - gap_ref[...].astype(jnp.float32), (stations, stations))
    here = lax.broadcasted_iota(jnp.int32, (stations, stations), 0)
    along = lax.broadcasted_iota(jnp.int32, (stations, stations), 1)
    kept = jnp.sum(jnp.where(here == along, kept, 0.0), axis=1, keepdims=True)
    factor = jnp.sqrt(SAMPLES / kept) / jnp.sqrt(power + 1e-06)
    white_ref[...] = (values * factor).astype(jnp.bfloat16) * LIFT


def into_bins(bins, corr_ref, out_ref):
    pairs = corr_ref.shape[0]
    count = out_ref.shape[0]
    for start in range(0, count, BIN_ROWS):
        ids = lax.broadcasted_iota(jnp.int32, (BIN_ROWS, pairs), 0) + start
        place = (ids == bins).astype(jnp.bfloat16)
        out_ref[start : start + BIN_ROWS, :] = jnp.dot(
            place, corr_ref[...], preferred_element_type=jnp.float32
        ).astype(out_ref.dtype)


def correlate_kernel(bins_ref, white_ref, first_ref, second_ref, table_ref, corr_ref, away_ref):
    pairs = corr_ref.shape[0]

    def pick(one_hot, rows):
        return jnp.dot(one_hot, rows, preferred_element_type=jnp.float32)

    def lags(cross, table):
        return lax.dot_general(
            cross, table, (((1,), (1,)), ((), ())), preferred_element_type=jnp.float32
        )

    for start in range(0, pairs, ROWS):
        rows = slice(start, start + ROWS)
        one, two = first_ref[rows, :], second_ref[rows, :]
        total = jnp.zeros((ROWS, LAGS), jnp.float32)
        for column in range(0, F, COLUMNS):
            here = slice(column, column + COLUMNS)
            real = white_ref[:, here]
            imag = white_ref[:, F + column : F + column + COLUMNS]
            real_one, imag_one = pick(one, real), pick(one, imag)
            real_two, imag_two = pick(two, real), pick(two, imag)
            cross = jnp.concatenate(
                [
                    (real_one * real_two + imag_one * imag_two).astype(jnp.bfloat16),
                    (imag_one * real_two - real_one * imag_two).astype(jnp.bfloat16),
                ],
                axis=1,
            )
            total += lags(cross, table_ref[:, 2 * column : 2 * column + 2 * COLUMNS])
        corr_ref[rows, :] = total.astype(jnp.bfloat16)
    into_bins(bins_ref[0:1, :], corr_ref, away_ref)


def own_kernel(bins_ref, corr_ref, out_ref):
    into_bins(bins_ref[1:2, :], corr_ref, out_ref)


def on_device(spectra, gap_counts, band_weight, pair_list, stack_owner, stack_slot):
    stations = spectra.shape[0]
    pairs = pair_list.shape[0]
    seg = lax.axis_size("seg")
    group = stations * lax.axis_size("grp")
    bins = seg // 2 * SLOTS_DEV
    inputs = (
        spectra, gap_counts.reshape(1, stations), pair_list.T, stack_owner.reshape(1, pairs),
        stack_slot.reshape(1, pairs), band_weight.reshape(1, F), *map(jnp.asarray, tables()),
    )
    white, first, second, bin_rows, table = pl.pallas_call(
        prepare_kernel,
        in_specs=[pl.BlockSpec(memory_space=pltpu.HBM)] * len(inputs),
        out_shape=[
            jax.ShapeDtypeStruct(spectra.shape, jnp.bfloat16),
            jax.ShapeDtypeStruct((pairs, group), jnp.bfloat16),
            jax.ShapeDtypeStruct((pairs, group), jnp.bfloat16),
            jax.ShapeDtypeStruct((2, pairs), jnp.int32),
            jax.ShapeDtypeStruct((LAGS, 2 * F), jnp.bfloat16),
        ],
        scratch_shapes=[pltpu.VMEM(x.shape, x.dtype) for x in inputs]
        + [pltpu.SemaphoreType.DMA((len(inputs),))],
        compiler_params=pltpu.CompilerParams(vmem_limit_bytes=16 * MIB),
    )(*[pltpu.with_memory_space_constraint(x, pltpu.HBM) for x in inputs])
    group_rows = lax.all_gather(white.astype(jnp.float16), "grp", axis=0, tiled=True).astype(jnp.bfloat16)

    corr, away = pl.pallas_call(
        correlate_kernel,
        out_shape=[
            jax.ShapeDtypeStruct((pairs, LAGS), jnp.bfloat16),
            jax.ShapeDtypeStruct((bins, LAGS), jnp.bfloat16),
        ],
        compiler_params=pltpu.CompilerParams(vmem_limit_bytes=16 * MIB),
    )(bin_rows, group_rows, first, second, table)
    arrived = lax.ppermute(away, "seg", [(i, i ^ 1) for i in range(seg)])
    kept = pl.pallas_call(
        own_kernel,
        out_shape=jax.ShapeDtypeStruct((bins, LAGS), jnp.float32),
        compiler_params=pltpu.CompilerParams(vmem_limit_bytes=8 * MIB),
        cost_estimate=pl.CostEstimate(flops=2 * bins * pairs * LAGS, bytes_accessed=2 << 20, transcendentals=0),
    )(bin_rows, corr)
    chip = (kept + arrived.astype(jnp.float32)).astype(jnp.bfloat16).reshape(seg // 2, SLOTS_DEV, LAGS)
    got = lax.all_to_all(
        chip, "seg", split_axis=0, concat_axis=0, tiled=True,
        axis_index_groups=[list(range(core, seg, 2)) for core in range(2)],
    )
    return jnp.sum(got.astype(jnp.float32), axis=0)


def solution(mesh):
    placed = (
        P(("grp", "seg"), None),
        P(("grp", "seg")),
        P(),
        P(("grp", "seg"), None),
        P(("grp", "seg"), None),
        P(("grp", "seg")),
    )
    return jax.shard_map(
        on_device, mesh=mesh, in_specs=placed, out_specs=P(("grp", "seg"), None), check_vma=False
    )
```

time: 79.5 us -> 80.2 us (level)
  Pallas kernels: 8.81 us -> 12 us
  local copies, waits for them, and re-layouts: 2.38 us -> 0 us
    pallas_call x1, Pallas kernels: 0.2 us -> 2.89 us  [on_device(): pl.pallas_call(prepare_kernel, in_specs=[pl.BlockSpec(memory_space=pltpu....]
    unnamed x20 -> x0, local copies, waits for them, and re-layouts: 2.38 us -> none
where the time goes in v6:
time: 80.2 us; the launch traced here: 79.6 us
  blocking collectives  63.4 us (79%)
  Pallas kernels  12 us (15%)
  starting transfers between devices  1.92 us (2%)
  waiting for transfers between devices  1.17 us (1%)
  other arithmetic  1.13 us (1%)
    all_gather x1, blocking collectives, on_device(): lax.all_gather(white.astype(jnp.float16), 'grp', axis=0, tiled=True)  36.3 us
    all_to_all x1, blocking collectives, on_device(): lax.all_to_all(chip, 'seg', split_axis=0, concat_axis=0, tiled=True, axis...  27.1 us
    pallas_call x1, Pallas kernels, on_device(): pl.pallas_call(correlate_kernel, out_shape=[jax.ShapeDtypeStruct((pairs,...  8.36 us
    pallas_call x1, Pallas kernels, on_device(): pl.pallas_call(prepare_kernel, in_specs=[pl.BlockSpec(memory_space=pltpu....  2.89 us
    ppermute x1, starting transfers between devices, on_device(): arrived = lax.ppermute(away, 'seg', [(i, i ^ 1) for i in range(seg)])  1.92 us
  transfers between devices with their start and end apart: 1, of which 1 were waited for; matrix products, arithmetic and copies ran while one was open for 0% of the time, Pallas kernels for 1%

profile of v6, /device:TPU:6, one launch (start us, length us, event | category | flops | bytes accessed | tf_op | source)
XLA Modules:
  0.0 79.6 jit_solution(16324480266720301355)
XLA Ops:
  0.0 2.9 %shard_map.82 = (bf16[32,4096]{1,0:T(8,128)(2,1)S(1)}, bf16[1024,256]{1,0:T(8,128)(2,1)S(1)}, bf16[1024,256]{1,0:T(8,128)(2,1)S(1)}, s32[2,1024]{1,0:T(2,128)S(1)}, bf16[256,4096]{1,0:T(8,128)(2,1)S(1)}) custom-call(bf16[32,4096]{1,0:T(8,128)(2,1)} %spectra_hbm.1, s32[1,32]{1,0:T(1,128)} %bitcast.11, s32[2,1024]{1,0:T(2,128)} %bitcast.7, s32[1,1024]{1,0:T(1,128)} %bitcast.9, ...), custom_call_target="tpu_custom_call" | custom-call | tf_op jit(solution)/shard_map/pallas_call | solution.py:140
  3.0 36.3 %all-gather.1 = f16[256,4096]{1,0:T(8,128)(2,1)S(1)} all-gather(f16[32,4096]{1,0:T(8,128)(2,1)S(1)} %convert_element_type.15), channel_id=1, replica_groups=mesh['grp'=8,'seg'=64] {'grp'}, dimensions={0}, use_global_device_ids=true | all-gather | bytes 2359296 | tf_op jit(solution)/shard_map/all_gather | solution.py:154
  39.2 0.3 convert_element_type.16.white_ref
  39.5 8.4 %shard_map.83 = (bf16[1024,256]{1,0:T(8,128)(2,1)S(1)}, bf16[1024,256]{1,0:T(8,128)(2,1)S(1)}) custom-call(s32[2,1024]{1,0:T(2,128)S(1)} %get-tuple-element.12.bins_ref, bf16[256,4096]{1,0:T(8,128)(2,1)S(1)} %convert_element_type.16.white_ref, bf16[1024,256]{1,0:T(8,128)(2,1)S(1)} %get-tuple-element.14.first_ref, ...), custom_call_target="tpu_custom_call" | custom-call | tf_op jit(solution)/shard_map/pallas_call | solution.py:156
  47.9 1.9 %collective-permute-start = (bf16[1024,256]{1,0:T(8,128)(2,1)S(1)}, bf16[1024,256]{1,0:T(8,128)(2,1)S(1)}, u32[]{:S(2)}, u32[]{:S(2)}) collective-permute-start(bf16[1024,256]{1,0:T(8,128)(2,1)S(1)} %get-tuple-element.18), channel_id=1, source_target_pairs={{0,1},{1,0},{2,3},{3,2},{4,5},{5,4},{6,7},{7,6},{8,9},{9,8},{10,11... | collective-permute-start | bytes 1572872 | tf_op jit(solution)/shard_map/ppermute | solution.py:164
  49.8 0.7 shard_map.84
  50.5 1.2 %collective-permute-done = bf16[1024,256]{1,0:T(8,128)(2,1)S(1)} collective-permute-done((bf16[1024,256]{1,0:T(8,128)(2,1)S(1)}, bf16[1024,256]{1,0:T(8,128)(2,1)S(1)}, u32[]{:S(2)}, u32[]{:S(2)}) %collective-permute-start) | collective-permute-done | bytes 524320 | tf_op jit(solution)/shard_map/ppermute | solution.py:164
  51.7 0.1 add_convert_fusion
  51.8 27.1 %all_to_all.5 = bf16[32,32,256]{2,1,0:T(8,128)(2,1)S(1)} all-to-all(bf16[32,32,256]{2,1,0:T(8,128)(2,1)S(1)} %bitcast.6), channel_id=1, replica_groups={{0,2,4,6,8,10,12,14,16,18,20,22,24,26,28,30,32,34,36,38,40,42,44,46,48,..., dimensions={0} | all-to-all | bytes 1048576 | tf_op jit(solution)/shard_map/all_to_all | solution.py:172
  78.9 0.7 convert_reduce_fusion
  (1 shorter events, 0.0 us)
Async XLA Ops:
  47.9 3.8 %collective-permute-start = (bf16[1024,256]{1,0:T(8,128)(2,1)S(1)}, bf16[1024,256]{1,0:T(8,128)(2,1)S(1)}, u32[]{:S(2)}, u32[]{:S(2)}) collective-permute-start(bf16[1024,256]{1,0:T(8,128)(2,1)S(1)} %get-tuple-element.18), channel_id=1, source_target_pairs={{0,1},{1,0},{2,3},{3,2},{4,5},{5,4},{6,7},{7,6},{8,9},{9,8},{10,11... | collective-permute-start | bytes 1572872 | tf_op jit(solution)/shard_map/ppermute | solution.py:164

commit v7 on v3

--- a/solution.py
+++ b/solution.py
@@ -14,9 +14,10 @@
 SLOTS_DEV = 32
 LIFT = 256.0
 FINE = 16
+SMALL = 6
 COLUMNS = 256
 ROWS = 512
-BIN_ROWS = 256
+BIN_ROWS = 128
 MIB = 1024 * 1024
 
 
@@ -25,10 +26,19 @@
     coarse = np.arange(0, LAGS, FINE, dtype=np.int64) - LAGS // 2
     fine = np.arange(FINE, dtype=np.int64)
     angles = [(k[:, None] * freqs[None, :]) % (2 * F) * (math.pi / F) for k in (coarse, fine)]
-    return [f(angle).astype(np.float32) for angle in angles for f in (np.cos, np.sin)]
+    return [np.concatenate([np.cos(angle), np.sin(angle)]).astype(np.float32) for angle in angles]
 
 
-def whiten_kernel(spectra_ref, gap_ref, out_ref):
+def whiten_kernel(*refs):
+    spectra_hbm, gap_hbm, *small_hbm = refs[: 2 + SMALL]
+    white_ref, *small_refs = refs[2 + SMALL : 3 + 2 * SMALL]
+    spectra_ref, gap_ref, sems = refs[3 + 2 * SMALL :]
+    moved = zip((spectra_hbm, gap_hbm, *small_hbm), (spectra_ref, gap_ref, *small_refs))
+    copies = [pltpu.make_async_copy(src, dst, sems.at[i]) for i, (src, dst) in enumerate(moved)]
+    for copy in copies:
+        copy.start()
+    for copy in copies[:2]:
+        copy.wait()
     stations = spectra_ref.shape[0]
     values = spectra_ref[...].astype(jnp.float32)
     power = jnp.mean(values * values, axis=1, keepdims=True)
@@ -37,7 +47,9 @@
     along = lax.broadcasted_iota(jnp.int32, (stations, stations), 1)
     kept = jnp.sum(jnp.where(here == along, kept, 0.0), axis=1, keepdims=True)
     factor = jnp.sqrt(SAMPLES / kept) / jnp.sqrt(power + 1e-06)
-    out_ref[...] = (values * factor).astype(jnp.bfloat16) * LIFT
+    white_ref[...] = (values * factor).astype(jnp.bfloat16) * LIFT
+    for copy in copies[2:]:
+        copy.wait()
 
 
 def pick_bins(owner_ref, slot_ref, parity):
@@ -58,7 +70,7 @@
 
 
 def correlate_kernel(
-    pairs_ref, owner_ref, slot_ref, white_ref, weight_ref, cos_ref, sin_ref, cos_fine_ref, sin_fine_ref,
+    pairs_ref, owner_ref, slot_ref, white_ref, weight_ref, coarse_ref, fine_ref,
     corr_ref, away_ref, first_ref, second_ref, table_ref,
 ):
     group = white_ref.shape[0]
@@ -67,15 +79,18 @@
     first_ref[...] = (ids == pairs_ref[0:1, :]).astype(jnp.float32).T.astype(jnp.bfloat16)
     second_ref[...] = (ids == pairs_ref[1:2, :]).astype(jnp.float32).T.astype(jnp.bfloat16)
     weight = weight_ref[...] * (0.25 / math.sqrt(F) / (LIFT * LIFT))
-    for lag in range(0, LAGS, FINE):
-        cos = weight * cos_ref[lag // FINE : lag // FINE + 1, :]
-        sin = weight * sin_ref[lag // FINE : lag // FINE + 1, :]
-        upper = (cos * cos_fine_ref[...] - sin * sin_fine_ref[...]).astype(jnp.bfloat16)
-        lower = (-(sin * cos_fine_ref[...] + cos * sin_fine_ref[...])).astype(jnp.bfloat16)
+    cos_fine, sin_fine = fine_ref[:FINE, :], fine_ref[FINE:, :]
+    blocks = LAGS // FINE
+    for block in range(blocks):
+        cos = weight * coarse_ref[block : block + 1, :]
+        sin = weight * coarse_ref[blocks + block : blocks + block + 1, :]
+        upper = (cos * cos_fine - sin * sin_fine).astype(jnp.bfloat16)
+        lower = (-(sin * cos_fine + cos * sin_fine)).astype(jnp.bfloat16)
+        rows = slice(block * FINE, block * FINE + FINE)
         for column in range(0, F, COLUMNS):
             here = slice(column, column + COLUMNS)
-            table_ref[lag : lag + FINE, 2 * column : 2 * column + COLUMNS] = upper[:, here]
-            table_ref[lag : lag + FINE, 2 * column + COLUMNS : 2 * column + 2 * COLUMNS] = lower[:, here]
+            table_ref[rows, 2 * column : 2 * column + COLUMNS] = upper[:, here]
+            table_ref[rows, 2 * column + COLUMNS : 2 * column + 2 * COLUMNS] = lower[:, here]
 
     def pick(one_hot, rows):
         return jnp.dot(one_hot, rows, preferred_element_type=jnp.float32)
@@ -119,15 +134,24 @@
     seg = lax.axis_size("seg")
     group = stations * lax.axis_size("grp")
     bins = seg // 2 * SLOTS_DEV
-    white = pl.pallas_call(
+    inputs = (
+        spectra, gap_counts.reshape(1, stations), pair_list.T, stack_owner.reshape(1, pairs),
+        stack_slot.reshape(1, pairs), band_weight.reshape(1, F), *map(jnp.asarray, tables()),
+    )
+    white, ends, owner, slot, weight, coarse, fine = pl.pallas_call(
         whiten_kernel,
-        out_shape=jax.ShapeDtypeStruct(spectra.shape, jnp.bfloat16),
+        in_specs=[pl.BlockSpec(memory_space=pltpu.HBM)] * len(inputs),
+        out_shape=[jax.ShapeDtypeStruct(spectra.shape, jnp.bfloat16)]
+        + [jax.ShapeDtypeStruct(x.shape, x.dtype) for x in inputs[2:]],
+        scratch_shapes=[
+            pltpu.VMEM(inputs[0].shape, inputs[0].dtype),
+            pltpu.VMEM(inputs[1].shape, inputs[1].dtype),
+            pltpu.SemaphoreType.DMA((len(inputs),)),
+        ],
         compiler_params=pltpu.CompilerParams(vmem_limit_bytes=8 * MIB),
-    )(spectra, gap_counts.reshape(1, stations))
+    )(*[pltpu.with_memory_space_constraint(x, pltpu.HBM) for x in inputs])
     group_rows = lax.all_gather(white.astype(jnp.float16), "grp", axis=0, tiled=True).astype(jnp.bfloat16)
 
-    owner = stack_owner.reshape(1, pairs)
-    slot = stack_slot.reshape(1, pairs)
     corr, away = pl.pallas_call(
         correlate_kernel,
         out_shape=[
@@ -141,7 +165,7 @@
         ],
         compiler_params=pltpu.CompilerParams(vmem_limit_bytes=24 * MIB),
     )(
-        pair_list.T, owner, slot, group_rows, band_weight.reshape(1, F), *tables()
+        ends, owner, slot, group_rows, weight, coarse, fine
     )
     arrived = lax.ppermute(away, "seg", [(i, i ^ 1) for i in range(seg)])
     kept = pl.pallas_call(

time: 79.5 us -> 78.1 us (0.982)
  local copies, waits for them, and re-layouts: 2.38 us -> 0 us
  Pallas kernels: 8.81 us -> 9.87 us
    unnamed x20 -> x0, local copies, waits for them, and re-layouts: 2.38 us -> none
    pallas_call x1, Pallas kernels: 0.2 us -> 1.26 us  [on_device(): pl.pallas_call(whiten_kernel, in_specs=[pl.BlockSpec(memory_space=pltpu.H...]
where the time goes in v7:
time: 78.1 us; the launch traced here: 77.5 us
  blocking collectives  63.4 us (81%)
  Pallas kernels  9.87 us (13%)
  starting transfers between devices  1.92 us (2%)
  waiting for transfers between devices  1.16 us (1%)
  other arithmetic  1.13 us (1%)
    all_gather x1, blocking collectives, on_device(): lax.all_gather(white.astype(jnp.float16), 'grp', axis=0, tiled=True)  36.3 us
    all_to_all x1, blocking collectives, on_device(): lax.all_to_all(chip, 'seg', split_axis=0, concat_axis=0, tiled=True, axis...  27.1 us
    pallas_call x1, Pallas kernels, on_device(): pl.pallas_call(correlate_kernel, out_shape=[jax.ShapeDtypeStruct((pairs,...  7.89 us
    ppermute x1, starting transfers between devices, on_device(): arrived = lax.ppermute(away, 'seg', [(i, i ^ 1) for i in range(seg)])  1.92 us
  transfers between devices with their start and end apart: 1, of which 1 were waited for; matrix products, arithmetic and copies ran while one was open for 0% of the time, Pallas kernels for 1%

profile of v7, /device:TPU:6, one launch (start us, length us, event | category | flops | bytes accessed | tf_op | source)
XLA Modules:
  0.0 77.5 jit_solution(16336875392167895487)
XLA Ops:
  0.0 1.3 %shard_map.82 = (bf16[32,4096]{1,0:T(8,128)(2,1)S(1)}, s32[2,1024]{1,0:T(2,128)S(1)}, s32[1,1024]{1,0:T(1,128)S(1)}, s32[1,1024]{1,0:T(1,128)S(1)}, f32[1,2048]{...) custom-call(bf16[32,4096]{1,0:T(8,128)(2,1)} %refs_0_.1, s32[1,32]{1,0:T(1,128)} %bitcast.11, ...), custom_call_target="tpu_custom_call" | custom-call | tf_op jit(solution)/shard_map/pallas_call | solution.py:141
  1.3 36.3 %all-gather.1 = f16[256,4096]{1,0:T(8,128)(2,1)S(1)} all-gather(f16[32,4096]{1,0:T(8,128)(2,1)S(1)} %convert_element_type.15), channel_id=1, replica_groups=mesh['grp'=8,'seg'=64] {'grp'}, dimensions={0}, use_global_device_ids=true | all-gather | bytes 2359296 | tf_op jit(solution)/shard_map/all_gather | solution.py:153
  37.6 0.3 convert_element_type.16.white_ref
  37.9 7.9 %shard_map.83 = (bf16[1024,256]{1,0:T(8,128)(2,1)S(1)}, bf16[1024,256]{1,0:T(8,128)(2,1)S(1)}) custom-call(s32[2,1024]{1,0:T(2,128)S(1)} %get-tuple-element.16.pairs_ref, s32[1,1024]{1,0:T(1,128)S(1)} %get-tuple-element.14.owner_ref, s32[1,1024]{1,0:T(1,128)S(1)} %get-tuple-element.15.slot_ref, bf16[256,4096]{1,0:T(8,128)(2,1)S(1)} %convert_element_type.16.white_ref, ...), custom_call_target="tpu_custom_call" | custom-call | tf_op jit(solution)/shard_map/pallas_call | solution.py:155
  45.8 1.9 %collective-permute-start = (bf16[1024,256]{1,0:T(8,128)(2,1)S(1)}, bf16[1024,256]{1,0:T(8,128)(2,1)S(1)}, u32[]{:S(2)}, u32[]{:S(2)}) collective-permute-start(bf16[1024,256]{1,0:T(8,128)(2,1)S(1)} %get-tuple-element.22), channel_id=1, source_target_pairs={{0,1},{1,0},{2,3},{3,2},{4,5},{5,4},{6,7},{7,6},{8,9},{9,8},{10,11... | collective-permute-start | bytes 1572872 | tf_op jit(solution)/shard_map/ppermute | solution.py:170
  47.7 0.7 shard_map.84
  48.4 1.2 %collective-permute-done = bf16[1024,256]{1,0:T(8,128)(2,1)S(1)} collective-permute-done((bf16[1024,256]{1,0:T(8,128)(2,1)S(1)}, bf16[1024,256]{1,0:T(8,128)(2,1)S(1)}, u32[]{:S(2)}, u32[]{:S(2)}) %collective-permute-start) | collective-permute-done | bytes 524320 | tf_op jit(solution)/shard_map/ppermute | solution.py:170
  49.6 0.1 add_convert_fusion
  49.7 27.1 %all_to_all.5 = bf16[32,32,256]{2,1,0:T(8,128)(2,1)S(1)} all-to-all(bf16[32,32,256]{2,1,0:T(8,128)(2,1)S(1)} %bitcast.6), channel_id=1, replica_groups={{0,2,4,6,8,10,12,14,16,18,20,22,24,26,28,30,32,34,36,38,40,42,44,46,48,..., dimensions={0} | all-to-all | bytes 1048576 | tf_op jit(solution)/shard_map/all_to_all | solution.py:178
  76.8 0.7 convert_reduce_fusion
  (1 shorter events, 0.0 us)
Async XLA Ops:
  45.8 3.8 %collective-permute-start = (bf16[1024,256]{1,0:T(8,128)(2,1)S(1)}, bf16[1024,256]{1,0:T(8,128)(2,1)S(1)}, u32[]{:S(2)}, u32[]{:S(2)}) collective-permute-start(bf16[1024,256]{1,0:T(8,128)(2,1)S(1)} %get-tuple-element.22), channel_id=1, source_target_pairs={{0,1},{1,0},{2,3},{3,2},{4,5},{5,4},{6,7},{7,6},{8,9},{9,8},{10,11... | collective-permute-start | bytes 1572872 | tf_op jit(solution)/shard_map/ppermute | solution.py:170

commit v8 on v7

--- a/solution.py
+++ b/solution.py
@@ -12,6 +12,7 @@
 LAGS = 256
 SAMPLES = 72000
 SLOTS_DEV = 32
+CHIPS_Y, CHIPS_X = 8, 4
 LIFT = 256.0
 FINE = 16
 SMALL = 6
@@ -52,9 +53,16 @@
         copy.wait()
 
 
+def far_first():
+    halves = [[k for i in range(n // 2) for k in (i, i + n // 2)] for n in (CHIPS_Y, CHIPS_X)]
+    return [y * CHIPS_X + x for y in halves[0] for x in halves[1]]
+
+
 def pick_bins(owner_ref, slot_ref, parity):
     owner = owner_ref[...]
-    local = (owner >> 1) * SLOTS_DEV + slot_ref[...]
+    y, x = owner // (2 * CHIPS_X), owner // 2 % CHIPS_X
+    place = (2 * (y % (CHIPS_Y // 2)) + y // (CHIPS_Y // 2)) * CHIPS_X + 2 * (x % 2) + x // 2
+    local = place * SLOTS_DEV + slot_ref[...]
     return jnp.where((owner & 1) == parity, local, -1)
 
 
@@ -177,7 +185,7 @@
     chip = (kept + arrived.astype(jnp.float32)).astype(jnp.bfloat16).reshape(seg // 2, SLOTS_DEV, LAGS)
     got = lax.all_to_all(
         chip, "seg", split_axis=0, concat_axis=0, tiled=True,
-        axis_index_groups=[list(range(core, seg, 2)) for core in range(2)],
+        axis_index_groups=[[2 * chip + core for chip in far_first()] for core in range(2)],
     )
     return jnp.sum(got.astype(jnp.float32), axis=0)
 

time: 78.1 us -> 79 us (1.012)
  the two profiles are of different devices: /device:TPU:6 before, /device:TPU:8 now
where the time goes in v8:
time: 79 us; the launch traced here: 78.8 us
  blocking collectives  64.7 us (82%)
  Pallas kernels  9.87 us (12%)
  starting transfers between devices  1.92 us (2%)
  waiting for transfers between devices  1.16 us (1%)
  other arithmetic  1.13 us (1%)
    all_gather x1, blocking collectives, on_device(): lax.all_gather(white.astype(jnp.float16), 'grp', axis=0, tiled=True)  36.3 us
    all_to_all x1, blocking collectives, on_device(): lax.all_to_all(chip, 'seg', split_axis=0, concat_axis=0, tiled=True, axis...  28.4 us
    pallas_call x1, Pallas kernels, on_device(): pl.pallas_call(correlate_kernel, out_shape=[jax.ShapeDtypeStruct((pairs,...  7.9 us
    ppermute x1, starting transfers between devices, on_device(): arrived = lax.ppermute(away, 'seg', [(i, i ^ 1) for i in range(seg)])  1.92 us
  transfers between devices with their start and end apart: 1, of which 1 were waited for; matrix products, arithmetic and copies ran while one was open for 0% of the time, Pallas kernels for 1%

profile of v8, /device:TPU:8, one launch (start us, length us, event | category | flops | bytes accessed | tf_op | source)
XLA Modules:
  0.0 78.8 jit_solution(13681175798800029414)
XLA Ops:
  0.0 1.3 %shard_map.82 = (bf16[32,4096]{1,0:T(8,128)(2,1)S(1)}, s32[2,1024]{1,0:T(2,128)S(1)}, s32[1,1024]{1,0:T(1,128)S(1)}, s32[1,1024]{1,0:T(1,128)S(1)}, f32[1,2048]{...) custom-call(bf16[32,4096]{1,0:T(8,128)(2,1)} %refs_0_.1, s32[1,32]{1,0:T(1,128)} %bitcast.11, ...), custom_call_target="tpu_custom_call" | custom-call | tf_op jit(solution)/shard_map/pallas_call | solution.py:149
  1.3 36.3 %all-gather.1 = f16[256,4096]{1,0:T(8,128)(2,1)S(1)} all-gather(f16[32,4096]{1,0:T(8,128)(2,1)S(1)} %convert_element_type.15), channel_id=1, replica_groups=mesh['grp'=8,'seg'=64] {'grp'}, dimensions={0}, use_global_device_ids=true | all-gather | bytes 2359296 | tf_op jit(solution)/shard_map/all_gather | solution.py:161
  37.6 0.3 convert_element_type.16.white_ref
  37.9 7.9 %shard_map.83 = (bf16[1024,256]{1,0:T(8,128)(2,1)S(1)}, bf16[1024,256]{1,0:T(8,128)(2,1)S(1)}) custom-call(s32[2,1024]{1,0:T(2,128)S(1)} %get-tuple-element.16.pairs_ref, s32[1,1024]{1,0:T(1,128)S(1)} %get-tuple-element.14.owner_ref, s32[1,1024]{1,0:T(1,128)S(1)} %get-tuple-element.15.slot_ref, bf16[256,4096]{1,0:T(8,128)(2,1)S(1)} %convert_element_type.16.white_ref, ...), custom_call_target="tpu_custom_call" | custom-call | tf_op jit(solution)/shard_map/pallas_call | solution.py:163
  45.8 1.9 %collective-permute-start = (bf16[1024,256]{1,0:T(8,128)(2,1)S(1)}, bf16[1024,256]{1,0:T(8,128)(2,1)S(1)}, u32[]{:S(2)}, u32[]{:S(2)}) collective-permute-start(bf16[1024,256]{1,0:T(8,128)(2,1)S(1)} %get-tuple-element.22), channel_id=1, source_target_pairs={{0,1},{1,0},{2,3},{3,2},{4,5},{5,4},{6,7},{7,6},{8,9},{9,8},{10,11... | collective-permute-start | bytes 1572872 | tf_op jit(solution)/shard_map/ppermute | solution.py:178
  47.7 0.7 shard_map.84
  48.4 1.2 %collective-permute-done = bf16[1024,256]{1,0:T(8,128)(2,1)S(1)} collective-permute-done((bf16[1024,256]{1,0:T(8,128)(2,1)S(1)}, bf16[1024,256]{1,0:T(8,128)(2,1)S(1)}, u32[]{:S(2)}, u32[]{:S(2)}) %collective-permute-start) | collective-permute-done | bytes 524320 | tf_op jit(solution)/shard_map/ppermute | solution.py:178
  49.6 0.1 add_convert_fusion
  49.7 28.4 %all_to_all.5 = bf16[32,32,256]{2,1,0:T(8,128)(2,1)S(1)} all-to-all(bf16[32,32,256]{2,1,0:T(8,128)(2,1)S(1)} %bitcast.6), channel_id=1, replica_groups={{0,4,2,6,32,36,34,38,8,12,10,14,40,44,42,46,16,20,18,22,48,52,50,54,24,..., dimensions={0} | all-to-all | bytes 1048576 | tf_op jit(solution)/shard_map/all_to_all | solution.py:186
  78.1 0.7 convert_reduce_fusion
  (1 shorter events, 0.0 us)
Async XLA Ops:
  45.8 3.8 %collective-permute-start = (bf16[1024,256]{1,0:T(8,128)(2,1)S(1)}, bf16[1024,256]{1,0:T(8,128)(2,1)S(1)}, u32[]{:S(2)}, u32[]{:S(2)}) collective-permute-start(bf16[1024,256]{1,0:T(8,128)(2,1)S(1)} %get-tuple-element.22), channel_id=1, source_target_pairs={{0,1},{1,0},{2,3},{3,2},{4,5},{5,4},{6,7},{7,6},{8,9},{9,8},{10,11... | collective-permute-start | bytes 1572872 | tf_op jit(solution)/shard_map/ppermute | solution.py:178

commit v9 on v7

--- a/solution.py
+++ b/solution.py
@@ -12,6 +12,7 @@
 LAGS = 256
 SAMPLES = 72000
 SLOTS_DEV = 32
+CHIPS = 32
 LIFT = 256.0
 FINE = 16
 SMALL = 6
@@ -54,7 +55,7 @@
 
 def pick_bins(owner_ref, slot_ref, parity):
     owner = owner_ref[...]
-    local = (owner >> 1) * SLOTS_DEV + slot_ref[...]
+    local = (CHIPS - 1 - (owner >> 1)) * SLOTS_DEV + slot_ref[...]
     return jnp.where((owner & 1) == parity, local, -1)
 
 
@@ -177,7 +178,7 @@
     chip = (kept + arrived.astype(jnp.float32)).astype(jnp.bfloat16).reshape(seg // 2, SLOTS_DEV, LAGS)
     got = lax.all_to_all(
         chip, "seg", split_axis=0, concat_axis=0, tiled=True,
-        axis_index_groups=[list(range(core, seg, 2)) for core in range(2)],
+        axis_index_groups=[list(range(core, seg, 2))[::-1] for core in range(2)],
     )
     return jnp.sum(got.astype(jnp.float32), axis=0)
 

time: 78.1 us -> 75.5 us (0.967)
  blocking collectives: 63.4 us -> 60.2 us
    all_to_all x1, blocking collectives: 27.1 us -> 23.9 us  [on_device(): lax.all_to_all(chip, 'seg', split_axis=0, concat_axis=0, tiled=True, axis...]
where the time goes in v9:
time: 75.5 us; the launch traced here: 74.3 us
  blocking collectives  60.2 us (80%)
  Pallas kernels  9.87 us (13%)
  starting transfers between devices  1.92 us (3%)
  waiting for transfers between devices  1.16 us (2%)
  other arithmetic  1.13 us (1%)
    all_gather x1, blocking collectives, on_device(): lax.all_gather(white.astype(jnp.float16), 'grp', axis=0, tiled=True)  36.3 us
    all_to_all x1, blocking collectives, on_device(): lax.all_to_all(chip, 'seg', split_axis=0, concat_axis=0, tiled=True, axis...  23.9 us
    pallas_call x1, Pallas kernels, on_device(): pl.pallas_call(correlate_kernel, out_shape=[jax.ShapeDtypeStruct((pairs,...  7.89 us
    ppermute x1, starting transfers between devices, on_device(): arrived = lax.ppermute(away, 'seg', [(i, i ^ 1) for i in range(seg)])  1.92 us
  transfers between devices with their start and end apart: 1, of which 1 were waited for; matrix products, arithmetic and copies ran while one was open for 0% of the time, Pallas kernels for 1%

profile of v9, /device:TPU:6, one launch (start us, length us, event | category | flops | bytes accessed | tf_op | source)
XLA Modules:
  0.0 74.3 jit_solution(16873703575179256839)
XLA Ops:
  0.0 1.3 %shard_map.82 = (bf16[32,4096]{1,0:T(8,128)(2,1)S(1)}, s32[2,1024]{1,0:T(2,128)S(1)}, s32[1,1024]{1,0:T(1,128)S(1)}, s32[1,1024]{1,0:T(1,128)S(1)}, f32[1,2048]{...) custom-call(bf16[32,4096]{1,0:T(8,128)(2,1)} %refs_0_.1, s32[1,32]{1,0:T(1,128)} %bitcast.11, ...), custom_call_target="tpu_custom_call" | custom-call | tf_op jit(solution)/shard_map/pallas_call | solution.py:142
  1.3 36.3 %all-gather.1 = f16[256,4096]{1,0:T(8,128)(2,1)S(1)} all-gather(f16[32,4096]{1,0:T(8,128)(2,1)S(1)} %convert_element_type.15), channel_id=1, replica_groups=mesh['grp'=8,'seg'=64] {'grp'}, dimensions={0}, use_global_device_ids=true | all-gather | bytes 2359296 | tf_op jit(solution)/shard_map/all_gather | solution.py:154
  37.6 0.3 convert_element_type.16.white_ref
  37.9 7.9 %shard_map.83 = (bf16[1024,256]{1,0:T(8,128)(2,1)S(1)}, bf16[1024,256]{1,0:T(8,128)(2,1)S(1)}) custom-call(s32[2,1024]{1,0:T(2,128)S(1)} %get-tuple-element.16.pairs_ref, s32[1,1024]{1,0:T(1,128)S(1)} %get-tuple-element.14.owner_ref, s32[1,1024]{1,0:T(1,128)S(1)} %get-tuple-element.15.slot_ref, bf16[256,4096]{1,0:T(8,128)(2,1)S(1)} %convert_element_type.16.white_ref, ...), custom_call_target="tpu_custom_call" | custom-call | tf_op jit(solution)/shard_map/pallas_call | solution.py:156
  45.8 1.9 %collective-permute-start = (bf16[1024,256]{1,0:T(8,128)(2,1)S(1)}, bf16[1024,256]{1,0:T(8,128)(2,1)S(1)}, u32[]{:S(2)}, u32[]{:S(2)}) collective-permute-start(bf16[1024,256]{1,0:T(8,128)(2,1)S(1)} %get-tuple-element.22), channel_id=1, source_target_pairs={{0,1},{1,0},{2,3},{3,2},{4,5},{5,4},{6,7},{7,6},{8,9},{9,8},{10,11... | collective-permute-start | bytes 1572872 | tf_op jit(solution)/shard_map/ppermute | solution.py:171
  47.7 0.7 shard_map.84
  48.4 1.2 %collective-permute-done = bf16[1024,256]{1,0:T(8,128)(2,1)S(1)} collective-permute-done((bf16[1024,256]{1,0:T(8,128)(2,1)S(1)}, bf16[1024,256]{1,0:T(8,128)(2,1)S(1)}, u32[]{:S(2)}, u32[]{:S(2)}) %collective-permute-start) | collective-permute-done | bytes 524320 | tf_op jit(solution)/shard_map/ppermute | solution.py:171
  49.6 0.1 add_convert_fusion
  49.7 23.9 %all_to_all.5 = bf16[32,32,256]{2,1,0:T(8,128)(2,1)S(1)} all-to-all(bf16[32,32,256]{2,1,0:T(8,128)(2,1)S(1)} %bitcast.6), channel_id=1, replica_groups={{62,60,58,56,54,52,50,48,46,44,42,40,38,36,34,32,30,28,26,24,22,20,18,1..., dimensions={0} | all-to-all | bytes 1048576 | tf_op jit(solution)/shard_map/all_to_all | solution.py:179
  73.6 0.7 convert_reduce_fusion
  (1 shorter events, 0.0 us)
Async XLA Ops:
  45.8 3.8 %collective-permute-start = (bf16[1024,256]{1,0:T(8,128)(2,1)S(1)}, bf16[1024,256]{1,0:T(8,128)(2,1)S(1)}, u32[]{:S(2)}, u32[]{:S(2)}) collective-permute-start(bf16[1024,256]{1,0:T(8,128)(2,1)S(1)} %get-tuple-element.22), channel_id=1, source_target_pairs={{0,1},{1,0},{2,3},{3,2},{4,5},{5,4},{6,7},{7,6},{8,9},{9,8},{10,11... | collective-permute-start | bytes 1572872 | tf_op jit(solution)/shard_map/ppermute | solution.py:171

commit v10 on v7

--- a/solution.py
+++ b/solution.py
@@ -12,6 +12,10 @@
 LAGS = 256
 SAMPLES = 72000
 SLOTS_DEV = 32
+ORDER = (
+    18, 19, 22, 23, 30, 31, 17, 21, 29, 26, 27, 16, 20, 28, 25, 14,
+    15, 10, 11, 13, 9, 24, 12, 6, 7, 8, 5, 2, 3, 1, 4, 0,
+)
 LIFT = 256.0
 FINE = 16
 SMALL = 6
@@ -54,7 +58,11 @@
 
 def pick_bins(owner_ref, slot_ref, parity):
     owner = owner_ref[...]
-    local = (owner >> 1) * SLOTS_DEV + slot_ref[...]
+    chip = owner >> 1
+    place = jnp.zeros_like(chip)
+    for position, number in enumerate(ORDER):
+        place = jnp.where(chip == number, position, place)
+    local = place * SLOTS_DEV + slot_ref[...]
     return jnp.where((owner & 1) == parity, local, -1)
 
 
@@ -177,7 +185,7 @@
     chip = (kept + arrived.astype(jnp.float32)).astype(jnp.bfloat16).reshape(seg // 2, SLOTS_DEV, LAGS)
     got = lax.all_to_all(
         chip, "seg", split_axis=0, concat_axis=0, tiled=True,
-        axis_index_groups=[list(range(core, seg, 2)) for core in range(2)],
+        axis_index_groups=[[2 * chip + core for chip in ORDER] for core in range(2)],
     )
     return jnp.sum(got.astype(jnp.float32), axis=0)
 

time: 78.1 us -> 74.2 us (0.950)
  blocking collectives: 63.4 us -> 59.9 us
    all_to_all x1, blocking collectives: 27.1 us -> 23.6 us  [on_device(): lax.all_to_all(chip, 'seg', split_axis=0, concat_axis=0, tiled=True, axis...]
where the time goes in v10:
time: 74.2 us; the launch traced here: 74 us
  blocking collectives  59.9 us (81%)
  Pallas kernels  9.86 us (13%)
  starting transfers between devices  1.92 us (3%)
  waiting for transfers between devices  1.16 us (2%)
  other arithmetic  1.13 us (2%)
    all_gather x1, blocking collectives, on_device(): lax.all_gather(white.astype(jnp.float16), 'grp', axis=0, tiled=True)  36.3 us
    all_to_all x1, blocking collectives, on_device(): lax.all_to_all(chip, 'seg', split_axis=0, concat_axis=0, tiled=True, axis...  23.6 us
    pallas_call x1, Pallas kernels, on_device(): pl.pallas_call(correlate_kernel, out_shape=[jax.ShapeDtypeStruct((pairs,...  7.9 us
    ppermute x1, starting transfers between devices, on_device(): arrived = lax.ppermute(away, 'seg', [(i, i ^ 1) for i in range(seg)])  1.92 us
  transfers between devices with their start and end apart: 1, of which 1 were waited for; matrix products, arithmetic and copies ran while one was open for 0% of the time, Pallas kernels for 1%

profile of v10, /device:TPU:6, one launch (start us, length us, event | category | flops | bytes accessed | tf_op | source)
XLA Modules:
  0.0 74.0 jit_solution(15786270935170003366)
XLA Ops:
  0.0 1.3 %shard_map.82 = (bf16[32,4096]{1,0:T(8,128)(2,1)S(1)}, s32[2,1024]{1,0:T(2,128)S(1)}, s32[1,1024]{1,0:T(1,128)S(1)}, s32[1,1024]{1,0:T(1,128)S(1)}, f32[1,2048]{...) custom-call(bf16[32,4096]{1,0:T(8,128)(2,1)} %refs_0_.1, s32[1,32]{1,0:T(1,128)} %bitcast.11, ...), custom_call_target="tpu_custom_call" | custom-call | tf_op jit(solution)/shard_map/pallas_call | solution.py:149
  1.3 36.3 %all-gather.1 = f16[256,4096]{1,0:T(8,128)(2,1)S(1)} all-gather(f16[32,4096]{1,0:T(8,128)(2,1)S(1)} %convert_element_type.15), channel_id=1, replica_groups=mesh['grp'=8,'seg'=64] {'grp'}, dimensions={0}, use_global_device_ids=true | all-gather | bytes 2359296 | tf_op jit(solution)/shard_map/all_gather | solution.py:161
  37.6 0.3 convert_element_type.16.white_ref
  37.9 7.9 %shard_map.83 = (bf16[1024,256]{1,0:T(8,128)(2,1)S(1)}, bf16[1024,256]{1,0:T(8,128)(2,1)S(1)}) custom-call(s32[2,1024]{1,0:T(2,128)S(1)} %get-tuple-element.16.pairs_ref, s32[1,1024]{1,0:T(1,128)S(1)} %get-tuple-element.14.owner_ref, s32[1,1024]{1,0:T(1,128)S(1)} %get-tuple-element.15.slot_ref, bf16[256,4096]{1,0:T(8,128)(2,1)S(1)} %convert_element_type.16.white_ref, ...), custom_call_target="tpu_custom_call" | custom-call | tf_op jit(solution)/shard_map/pallas_call | solution.py:163
  45.8 1.9 %collective-permute-start = (bf16[1024,256]{1,0:T(8,128)(2,1)S(1)}, bf16[1024,256]{1,0:T(8,128)(2,1)S(1)}, u32[]{:S(2)}, u32[]{:S(2)}) collective-permute-start(bf16[1024,256]{1,0:T(8,128)(2,1)S(1)} %get-tuple-element.22), channel_id=1, source_target_pairs={{0,1},{1,0},{2,3},{3,2},{4,5},{5,4},{6,7},{7,6},{8,9},{9,8},{10,11... | collective-permute-start | bytes 1572872 | tf_op jit(solution)/shard_map/ppermute | solution.py:178
  47.7 0.7 shard_map.84
  48.4 1.2 %collective-permute-done = bf16[1024,256]{1,0:T(8,128)(2,1)S(1)} collective-permute-done((bf16[1024,256]{1,0:T(8,128)(2,1)S(1)}, bf16[1024,256]{1,0:T(8,128)(2,1)S(1)}, u32[]{:S(2)}, u32[]{:S(2)}) %collective-permute-start) | collective-permute-done | bytes 524320 | tf_op jit(solution)/shard_map/ppermute | solution.py:178
  49.6 0.1 add_convert_fusion
  49.7 23.6 %all_to_all.5 = bf16[32,32,256]{2,1,0:T(8,128)(2,1)S(1)} all-to-all(bf16[32,32,256]{2,1,0:T(8,128)(2,1)S(1)} %bitcast.6), channel_id=1, replica_groups={{36,38,44,46,60,62,34,42,58,52,54,32,40,56,50,28,30,20,22,26,18,48,24,1..., dimensions={0} | all-to-all | bytes 1048576 | tf_op jit(solution)/shard_map/all_to_all | solution.py:186
  73.3 0.7 convert_reduce_fusion
  (1 shorter events, 0.0 us)
Async XLA Ops:
  45.8 3.8 %collective-permute-start = (bf16[1024,256]{1,0:T(8,128)(2,1)S(1)}, bf16[1024,256]{1,0:T(8,128)(2,1)S(1)}, u32[]{:S(2)}, u32[]{:S(2)}) collective-permute-start(bf16[1024,256]{1,0:T(8,128)(2,1)S(1)} %get-tuple-element.22), channel_id=1, source_target_pairs={{0,1},{1,0},{2,3},{3,2},{4,5},{5,4},{6,7},{7,6},{8,9},{9,8},{10,11... | collective-permute-start | bytes 1572872 | tf_op jit(solution)/shard_map/ppermute | solution.py:178

commit v11 on v10

--- a/solution.py
+++ b/solution.py
@@ -101,7 +101,7 @@
             table_ref[rows, 2 * column + COLUMNS : 2 * column + 2 * COLUMNS] = lower[:, here]
 
     def pick(one_hot, rows):
-        return jnp.dot(one_hot, rows, preferred_element_type=jnp.float32)
+        return jnp.dot(one_hot, rows, preferred_element_type=jnp.float32).astype(jnp.bfloat16)
 
     def lags(cross, table):
         return lax.dot_general(

time: 74.2 us -> 74 us (level)
  no operation moved by 1% of the time
where the time goes in v11:
time: 74 us; the launch traced here: 73.8 us
  blocking collectives  59.9 us (81%)
  Pallas kernels  9.7 us (13%)
  starting transfers between devices  1.92 us (3%)
  waiting for transfers between devices  1.16 us (2%)
  other arithmetic  1.13 us (2%)
    all_gather x1, blocking collectives, on_device(): lax.all_gather(white.astype(jnp.float16), 'grp', axis=0, tiled=True)  36.3 us
    all_to_all x1, blocking collectives, on_device(): lax.all_to_all(chip, 'seg', split_axis=0, concat_axis=0, tiled=True, axis...  23.6 us
    pallas_call x1, Pallas kernels, on_device(): pl.pallas_call(correlate_kernel, out_shape=[jax.ShapeDtypeStruct((pairs,...  7.73 us
    ppermute x1, starting transfers between devices, on_device(): arrived = lax.ppermute(away, 'seg', [(i, i ^ 1) for i in range(seg)])  1.92 us
  transfers between devices with their start and end apart: 1, of which 1 were waited for; matrix products, arithmetic and copies ran while one was open for 0% of the time, Pallas kernels for 1%

profile of v11, /device:TPU:6, one launch (start us, length us, event | category | flops | bytes accessed | tf_op | source)
XLA Modules:
  0.0 73.8 jit_solution(5897700135012225831)
XLA Ops:
  0.0 1.3 %shard_map.82 = (bf16[32,4096]{1,0:T(8,128)(2,1)S(1)}, s32[2,1024]{1,0:T(2,128)S(1)}, s32[1,1024]{1,0:T(1,128)S(1)}, s32[1,1024]{1,0:T(1,128)S(1)}, f32[1,2048]{...) custom-call(bf16[32,4096]{1,0:T(8,128)(2,1)} %refs_0_.1, s32[1,32]{1,0:T(1,128)} %bitcast.11, ...), custom_call_target="tpu_custom_call" | custom-call | tf_op jit(solution)/shard_map/pallas_call | solution.py:149
  1.3 36.3 %all-gather.1 = f16[256,4096]{1,0:T(8,128)(2,1)S(1)} all-gather(f16[32,4096]{1,0:T(8,128)(2,1)S(1)} %convert_element_type.15), channel_id=1, replica_groups=mesh['grp'=8,'seg'=64] {'grp'}, dimensions={0}, use_global_device_ids=true | all-gather | bytes 2359296 | tf_op jit(solution)/shard_map/all_gather | solution.py:161
  37.6 0.3 convert_element_type.16.white_ref
  37.9 7.7 %shard_map.83 = (bf16[1024,256]{1,0:T(8,128)(2,1)S(1)}, bf16[1024,256]{1,0:T(8,128)(2,1)S(1)}) custom-call(s32[2,1024]{1,0:T(2,128)S(1)} %get-tuple-element.16.pairs_ref, s32[1,1024]{1,0:T(1,128)S(1)} %get-tuple-element.14.owner_ref, s32[1,1024]{1,0:T(1,128)S(1)} %get-tuple-element.15.slot_ref, bf16[256,4096]{1,0:T(8,128)(2,1)S(1)} %convert_element_type.16.white_ref, ...), custom_call_target="tpu_custom_call" | custom-call | tf_op jit(solution)/shard_map/pallas_call | solution.py:163
  45.6 1.9 %collective-permute-start = (bf16[1024,256]{1,0:T(8,128)(2,1)S(1)}, bf16[1024,256]{1,0:T(8,128)(2,1)S(1)}, u32[]{:S(2)}, u32[]{:S(2)}) collective-permute-start(bf16[1024,256]{1,0:T(8,128)(2,1)S(1)} %get-tuple-element.22), channel_id=1, source_target_pairs={{0,1},{1,0},{2,3},{3,2},{4,5},{5,4},{6,7},{7,6},{8,9},{9,8},{10,11... | collective-permute-start | bytes 1572872 | tf_op jit(solution)/shard_map/ppermute | solution.py:178
  47.6 0.7 shard_map.84
  48.3 1.2 %collective-permute-done = bf16[1024,256]{1,0:T(8,128)(2,1)S(1)} collective-permute-done((bf16[1024,256]{1,0:T(8,128)(2,1)S(1)}, bf16[1024,256]{1,0:T(8,128)(2,1)S(1)}, u32[]{:S(2)}, u32[]{:S(2)}) %collective-permute-start) | collective-permute-done | bytes 524320 | tf_op jit(solution)/shard_map/ppermute | solution.py:178
  49.4 0.1 add_convert_fusion
  49.6 23.6 %all_to_all.5 = bf16[32,32,256]{2,1,0:T(8,128)(2,1)S(1)} all-to-all(bf16[32,32,256]{2,1,0:T(8,128)(2,1)S(1)} %bitcast.6), channel_id=1, replica_groups={{36,38,44,46,60,62,34,42,58,52,54,32,40,56,50,28,30,20,22,26,18,48,24,1..., dimensions={0} | all-to-all | bytes 1048576 | tf_op jit(solution)/shard_map/all_to_all | solution.py:186
  73.1 0.7 convert_reduce_fusion
  (1 shorter events, 0.0 us)
Async XLA Ops:
  45.6 3.8 %collective-permute-start = (bf16[1024,256]{1,0:T(8,128)(2,1)S(1)}, bf16[1024,256]{1,0:T(8,128)(2,1)S(1)}, u32[]{:S(2)}, u32[]{:S(2)}) collective-permute-start(bf16[1024,256]{1,0:T(8,128)(2,1)S(1)} %get-tuple-element.22), channel_id=1, source_target_pairs={{0,1},{1,0},{2,3},{3,2},{4,5},{5,4},{6,7},{7,6},{8,9},{9,8},{10,11... | collective-permute-start | bytes 1572872 | tf_op jit(solution)/shard_map/ppermute | solution.py:178
